TPU v7x, 32 devices: a whole 2x2x4 slice. The times are simulated.
32 devices in a mesh: sec: 2 (over y), sp: 4 (over x, core), dp: 4 (over z).
Axes of the slice: x: 2, y: 2, z: 4, core: 2. Of those that a mesh axis runs over, the one named last changes fastest.
Arguments:
- fraction: float32 [4, 8, 32, 1024], P('dp', None, 'sp', 'sec'), may hold values from 0 to 1
- labels: int32 [4, 8, 32, 1024], P('dp', ('sec', 'sp')), may hold values from 0 to 63
- conv_weight: bfloat16 [54, 64], replicated, may hold values from -6 to 6
- conv_bias: float32 [64], replicated, may hold values from -6 to 6
- out_weight: bfloat16 [64, 64], replicated, may hold values from -6 to 6
- out_bias: float32 [64], replicated, may hold values from -6 to 6
Outputs:
- cell_loss: float32 [4, 8, 32, 1024], P('dp', ('sec', 'sp'))
- conv_weight_grad: float32 [54, 64], replicated
- conv_bias_grad: float32 [64], replicated
- out_weight_grad: float32 [64, 64], replicated
- out_bias_grad: float32 [64], replicated
All inputs are finite; a program needn't handle non-finite values.
Results may differ from a plain program's by a relative error of at most 0.00035.
The roundings to bfloat16 on the way count: a program that leaves them out, or rounds other values in their place, can miss the bound.
Values may be sent and summed in bfloat16 or wider, within the bound.
No kernel may reach another device: no remote copies, remote signals or barrier semaphores. Data moves between devices by JAX's collectives and lax.ppermute only.
A program may use at most 64 MiB of HBM per device.

v0:
```python
import jax
import jax.numpy as jnp
from jax import lax
from jax.sharding import PartitionSpec as P

PY = 32
PZ = 32


def extended(cells, sides, width):
    for axis, dim in sides:
        count = lax.axis_size(axis)
        ends = count - 1
        head = lax.slice_in_dim(cells, 0, width, axis=dim)
        tail = lax.slice_in_dim(cells, cells.shape[dim] - width, cells.shape[dim], axis=dim)
        cells = jnp.concatenate(
            [
                lax.ppermute(tail, axis, [(i, (i + 1) % count) for i in range(ends)]),
                cells,
                lax.ppermute(head, axis, [((i + 1) % count, i) for i in range(ends)]),
            ],
            axis=dim,
        )
    return cells


def shift_cells(values, offset, step_y, step_z):
    length = values.shape[-1]
    margin = PY * PZ + PZ + 1
    widths = [(0, 0)] * (values.ndim - 1) + [(margin, margin)]
    padded = jnp.pad(values, widths)
    shifted = lax.slice_in_dim(
        padded, margin + offset, margin + offset + length, axis=values.ndim - 1
    )
    position = jnp.arange(length, dtype=jnp.int32)
    row_y = position // PZ % PY + step_y
    col_z = position % PZ + step_z
    inside = (row_y >= 0) & (row_y < PY) & (col_z >= 0) & (col_z < PZ)
    return jnp.where(inside, shifted, jnp.zeros((), values.dtype))


def brick_box(rimmed):
    x_sums = rimmed[:, :-2] + rimmed[:, 1:-1] + rimmed[:, 2:]
    y_sums = x_sums[:, :, :-2] + x_sums[:, :, 1:-1] + x_sums[:, :, 2:]
    z_padded = jnp.pad(y_sums, ((0, 0), (0, 0), (0, 0), (1, 1)))
    z_sums = z_padded[..., :-2] + z_padded[..., 1:-1] + z_padded[..., 2:]
    return z_sums / 27.0


def joint_layout(arrived, sections):
    channels, patches, planes, width = arrived.shape
    split = arrived.reshape(channels, patches, sections, planes // sections, width)
    ordered = split.transpose(0, 1, 3, 2, 4)
    return ordered.reshape(channels, patches, planes // sections, sections * width)


def relay_features(block):
    arrived = lax.all_to_all(block, ("sec", "sp"), split_axis=1, concat_axis=2, tiled=True)
    result = joint_layout(arrived, lax.axis_size("sec"))
    return result


def make_columns(features):
    shifted_list = []
    for step_x in (-1, 0, 1):
        for step_y in (-1, 0, 1):
            for step_z in (-1, 0, 1):
                offset = step_x * PY * PZ + step_y * PZ + step_z
                shifted_list.append(shift_cells(features, offset, step_y, step_z))
    stacked = jnp.stack(shifted_list)
    return stacked.reshape(2 * stacked.shape[0], stacked.shape[2])


def patch_step(features, patch_labels, conv_weight, conv_bias, out_weight, out_bias, weight_scale):
    columns = make_columns(features)
    hidden_pre = (
        jnp.einsum("kc,kh->hc", columns, conv_weight, preferred_element_type=jnp.float32)
        + conv_bias[:, None]
    )
    hidden_act = jax.nn.silu(hidden_pre).astype(jnp.bfloat16)
    logits = (
        jnp.einsum("hb,hc->bc", out_weight, hidden_act, preferred_element_type=jnp.float32)
        + out_bias[:, None]
    )
    exp_logits = jnp.exp(logits)
    partition = jnp.sum(exp_logits, axis=0)
    bin_ids = jnp.arange(logits.shape[0], dtype=jnp.int32)[:, None]
    is_label = bin_ids == patch_labels[None, :]
    cell_term = jnp.log(partition) - jnp.sum(jnp.where(is_label, logits, 0.0), axis=0)
    residual = (exp_logits / partition - is_label.astype(jnp.float32)) * weight_scale
    residual_low = residual.astype(jnp.bfloat16)
    out_weight_grad = jnp.einsum(
        "hc,bc->hb", hidden_act, residual_low, preferred_element_type=jnp.float32
    )
    out_bias_grad = jnp.sum(residual, axis=1)
    hidden_back = jnp.einsum(
        "hb,bc->hc", out_weight, residual_low, preferred_element_type=jnp.float32
    )
    sigmoid_pre = jax.nn.sigmoid(hidden_pre)
    hidden_grad = hidden_back * sigmoid_pre * (1.0 + hidden_pre * (1.0 - sigmoid_pre))
    conv_bias_grad = jnp.sum(hidden_grad, axis=1)
    hidden_low = hidden_grad.astype(jnp.bfloat16)
    conv_weight_grad = jnp.einsum(
        "kc,hc->kh", columns, hidden_low, preferred_element_type=jnp.float32
    )
    return (cell_term, (conv_weight_grad, conv_bias_grad, out_weight_grad, out_bias_grad))


def shards(fraction, labels, conv_weight, conv_bias, out_weight, out_bias):
    brick = fraction[0]
    patch_total, plane_count, row_width = brick.shape
    cubic = brick.reshape(patch_total, plane_count, row_width // PZ, PZ)
    rimmed = extended(cubic, (("sec", 2), ("sp", 1)), 1)
    filt = brick_box(rimmed)
    filt_sq = brick_box(rimmed * rimmed)
    local_feats = jnp.stack([filt, filt_sq - filt * filt]).astype(jnp.bfloat16)
    local_feats = local_feats.reshape(2, patch_total, plane_count, row_width)
    arrived = relay_features(local_feats)
    features = arrived.transpose(1, 0, 2, 3)
    patch_count = features.shape[0]
    features = features.reshape(patch_count, 2, -1)
    flat_labels = labels[0].reshape(patch_count, -1)
    cell_count = flat_labels.shape[1]
    weight_scale = 1.0 / (
        lax.axis_size("sec") * lax.axis_size("sp") * lax.axis_size("dp") * patch_count * cell_count
    )
    cell_term, terms = patch_step(
        features[0], flat_labels[0], conv_weight, conv_bias, out_weight, out_bias, weight_scale
    )
    conv_wsum = terms[0]
    conv_bsum = terms[1]
    out_wsum = terms[2]
    out_bsum = terms[3]
    losses = [cell_term]
    summed = lax.psum((conv_wsum, conv_bsum, out_wsum, out_bsum), ("sec", "sp", "dp"))
    cell_loss = jnp.stack(losses).reshape(labels.shape)
    return (cell_loss, summed[0], summed[1], summed[2], summed[3])


def solution(mesh):
    placed = (P("dp", None, "sp", "sec"), P("dp", ("sec", "sp"), None, None), P(), P(), P(), P())
    return jax.shard_map(
        shards,
        mesh=mesh,
        in_specs=placed,
        out_specs=(P("dp", ("sec", "sp"), None, None), P(), P(), P(), P()),
        check_vma=False,
    )
```

profile of v0, /device:TPU:0, one launch (start us, length us, event | category | flops | bytes accessed | tf_op | source)
XLA Modules:
  0.0 134.9 jit_solution(17039568145889468140)
XLA Ops:
  0.6 1.1 reshape_squeeze.3
  1.8 4.9 %collective-permute-start = (f32[8,8,1,32]{3,2,1,0:T(1,128)S(1)}, f32[8,8,1,32]{3,2,1,0:T(1,128)S(1)}, u32[]{:S(2)}, u32[]{:S(2)}) collective-permute-start(f32[8,8,1,32]{3,2,1,0:T(1,128)S(1)} %get-tuple-element.15), channel_id=1, source_target_pairs={{0,16},{1,17},{2,18},{3,19},{4,20},{5,21},{6,22},{7,23},{8,24},{9,... | collective-permute-start | bytes 24584 | tf_op jit(solution)/shard_map/ppermute | solution.py:18
  6.7 1.3 collective-permute-start.1
  8.4 4.1 %collective-permute-done.1 = f32[8,8,1,32]{3,2,1,0:T(1,128)S(1)} collective-permute-done((f32[8,8,1,32]{3,2,1,0:T(1,128)S(1)}, f32[8,8,1,32]{3,2,1,0:T(1,128)S(1)}, u32[]{:S(2)}, u32[]{:S(2)}) %collective-permute-start.1) | collective-permute-done | bytes 8224 | tf_op jit(solution)/shard_map/ppermute | solution.py:20
  12.7 1.3 collective-permute-start.2
  14.0 1.3 collective-permute-start.3
  15.3 3.6 %collective-permute-done.3 = f32[8,1,18,32]{3,2,1,0:T(8,128)S(1)} collective-permute-done((f32[8,1,18,32]{3,2,1,0:T(8,128)S(1)}, f32[8,1,18,32]{3,2,1,0:T(8,128)S(1)}, u32[]{:S(2)}, u32[]{:S(2)}) %collective-permute-start.3) | collective-permute-done | bytes 18464 | tf_op jit(solution)/shard_map/ppermute | solution.py:20
  21.6 4.5 %all-to-all-start = ((bf16[2,8,8,512]{3,2,0,1:T(8,128)(2,1)}), bf16[2,8,8,512]{3,2,0,1:T(8,128)(2,1)S(1)}, u32[]{:S(2)}, u32[]{:S(2)}) async-start(bf16[2,8,8,512]{3,2,0,1:T(8,128)(2,1)} %pad_maximum_fusion.7), calls=%async_computation | async-start | bytes 262144 | tf_op jit(solution)/shard_map/all_to_all | solution.py:58
  26.2 5.4 %all-to-all-done = bf16[2,8,8,512]{3,2,0,1:T(8,128)(2,1)S(1)} async-done(((bf16[2,8,8,512]{3,2,0,1:T(8,128)(2,1)}), bf16[2,8,8,512]{3,2,0,1:T(8,128)(2,1)S(1)}, u32[]{:S(2)}, u32[]{:S(2)}) %all-to-all-start) | async-done | bytes 131104 | tf_op jit(solution)/shard_map/all_to_all | solution.py:58
  34.9 1.0 fusion.37
  41.4 1.0 fusion.27
  43.4 1.0 fusion.39
  45.2 1.0 fusion.49
  46.1 1.0 fusion.55
  47.1 1.0 fusion.61
  53.7 1.0 fusion.51
  57.5 8.6 %reshape.84 = bf16[54,32768]{1,0:T(8,128)(2,1)} reshape(bf16[27,2,32768]{2,1,0:T(2,128)(2,1)} %fusion.69) | data formatting | bytes 7077888 | tf_op jit(solution)/shard_map/reshape | solution.py:71
  66.1 3.3 %fusion = f32[64,32768]{1,0:T(8,128)S(1)} fusion(bf16[54,32768]{1,0:T(8,128)(2,1)} %reshape.84, bf16[54,64]{1,0:T(8,128)(2,1)S(1)} %copy-done.2, f32[64]{0:T(128)S(1)} %copy-done.3), kind=kOutput, calls=%fused_computation.2 | convolution fusion | flops 228589568 | bytes 11934720 | tf_op jit(solution)/shard_map/kc,kh->hc/dot_general | solution.py:77
  69.5 4.1 %exponential_reduce_fusion = (f32[32768]{0:T(1024)S(1)}, f32[64,32768]{1,0:T(8,128)S(1)}) fusion(f32[64]{0:T(128)S(1)} %copy-done.4, bf16[64,64]{1,0:T(8,128)(2,1)S(1)} %copy-done, f32[64,32768]{1,0:T(8,128)S(1)} %fusion), kind=kOutput, calls=%fused_computation.12 | convolution fusion | flops 283082752 | bytes 16916736 | tf_op jit(solution)/shard_map/hb,hc->bc/dot_general | solution.py:82
  73.5 3.7 %fusion.6 = f32[64,64]{1,0:T(8,128)S(1)} fusion(f32[64,32768]{1,0:T(8,128)S(1)} %fusion, f32[64,32768]{1,0:T(8,128)S(1)} %get-tuple-element.18, f32[32768]{0:T(1024)S(1)} %get-tuple-element.17, s32[32768]{0:T(1024)S(1)} %bitcast.135), kind=kOutput, calls=%fused_computation.15 | convolution fusion | flops 291504128 | bytes 17055744 | tf_op jit(solution)/shard_map/hc,bc->hb/dot_general | solution.py:92
  77.2 7.4 %fusion.84 = (f32[64]{0:T(128)S(1)}, bf16[64,32768]{1,0:T(8,128)(2,1)}) fusion(f32[64,32768]{1,0:T(8,128)S(1)} %fusion, bf16[64,64]{1,0:T(8,128)(2,1)S(1)} %copy-done, s32[32768]{0:T(1024)S(1)} %bitcast.136, f32[32768]{0:T(1024)S(1)} %get-tuple-element.17, f32[64,32768]{1,0:T(8,128)S(1)} %get-tuple-element.18), kind=kOutput, calls=%fused_computation.157 | convolution fusion | flops 301989824 | bytes 21242112 | tf_op jit(solution)/shard_map/hb,bc->hc/dot_general | solution.py:96
  84.6 4.3 %fusion.81 = (f32[64]{0:T(128)S(1)}, f32[32768]{0:T(1024)S(1)}) fusion(s32[32768]{0:T(1024)S(1)} %bitcast.137, f32[32768]{0:T(1024)S(1)} %get-tuple-element.17, f32[64,32768]{1,0:T(8,128)S(1)} %get-tuple-element.18), kind=kLoop, calls=%fused_computation.154 | loop fusion | flops 16744384 | bytes 8782080 | tf_op jit(solution)/shard_map/reduce_sum | solution.py:95
  89.7 4.5 %fusion.4 = f32[54,64]{1,0:T(8,128)S(1)} fusion(bf16[54,32768]{1,0:T(8,128)(2,1)} %reshape.84, bf16[64,32768]{1,0:T(8,128)(2,1)} %get-tuple-element.20), kind=kOutput, calls=%fused_computation.13 | convolution fusion | flops 226492416 | bytes 7747072 | tf_op jit(solution)/shard_map/kc,hc->kh/dot_general | solution.py:103
  94.2 40.7 %all-reduce.3 = (f32[54,64]{1,0:T(8,128)}, f32[64]{0:T(128)}, f32[64,64]{1,0:T(8,128)}, f32[64]{0:T(128)}) all-reduce(f32[54,64]{1,0:T(8,128)S(1)} %fusion.4, f32[64]{0:T(128)S(1)} %get-tuple-element.19, f32[64,64]{1,0:T(8,128)S(1)} %fusion.6, f32[64]{0:T(128)S(1)} %get-tuple-element.5), channel_id=1, replica_groups=mesh['sec'=2,'sp'=4,'dp'=4] {'sec','sp','dp'}, use_global_device_ids=true, to_apply=%region_2.3 | all-reduce | flops 7680 | bytes 61440 | tf_op jit(solution)/shard_map/psum | solution.py:135
  (59 shorter events, 23.2 us)
Async XLA Ops:
  0.6 68.8 %copy-start = (bf16[64,64]{1,0:T(8,128)(2,1)S(1)}, bf16[64,64]{1,0:T(8,128)(2,1)}, u32[]{:S(2)}) copy-start(bf16[64,64]{1,0:T(8,128)(2,1)} %param.10) | copy-start | bytes 24580
  1.8 6.6 %collective-permute-start = (f32[8,8,1,32]{3,2,1,0:T(1,128)S(1)}, f32[8,8,1,32]{3,2,1,0:T(1,128)S(1)}, u32[]{:S(2)}, u32[]{:S(2)}) collective-permute-start(f32[8,8,1,32]{3,2,1,0:T(1,128)S(1)} %get-tuple-element.15), channel_id=1, source_target_pairs={{0,16},{1,17},{2,18},{3,19},{4,20},{5,21},{6,22},{7,23},{8,24},{9,... | collective-permute-start | bytes 24584 | tf_op jit(solution)/shard_map/ppermute | solution.py:18
  6.7 5.8 %collective-permute-start.1 = (f32[8,8,1,32]{3,2,1,0:T(1,128)S(1)}, f32[8,8,1,32]{3,2,1,0:T(1,128)S(1)}, u32[]{:S(2)}, u32[]{:S(2)}) collective-permute-start(f32[8,8,1,32]{3,2,1,0:T(1,128)S(1)} %get-tuple-element.16), channel_id=1, source_target_pairs={{16,0},{17,1},{18,2},{19,3},{20,4},{21,5},{22,6},{23,7},{24,8},{25... | collective-permute-start | bytes 24584 | tf_op jit(solution)/shard_map/ppermute | solution.py:20
  12.7 2.7 %collective-permute-start.2 = (f32[8,1,18,32]{3,2,1,0:T(8,128)S(1)}, f32[8,1,18,32]{3,2,1,0:T(8,128)S(1)}, u32[]{:S(2)}, u32[]{:S(2)}) collective-permute-start(f32[8,1,18,32]{3,2,1,0:T(8,128)S(1)} %get-tuple-element.11), channel_id=1, source_target_pairs={{0,4},{4,8},{8,12},{1,5},{5,9},{9,13},{2,6},{6,10},{10,14},{3,7},{... | collective-permute-start | bytes 55304 | tf_op jit(solution)/shard_map/ppermute | solution.py:18
  14.0 4.9 %collective-permute-start.3 = (f32[8,1,18,32]{3,2,1,0:T(8,128)S(1)}, f32[8,1,18,32]{3,2,1,0:T(8,128)S(1)}, u32[]{:S(2)}, u32[]{:S(2)}) collective-permute-start(f32[8,1,18,32]{3,2,1,0:T(8,128)S(1)} %get-tuple-element.12), channel_id=1, source_target_pairs={{4,0},{8,4},{12,8},{5,1},{9,5},{13,9},{6,2},{10,6},{14,10},{7,3},{... | collective-permute-start | bytes 55304 | tf_op jit(solution)/shard_map/ppermute | solution.py:20
  19.4 6.8 %copy-start.1 = (s32[1,1,32,1024]{3,2,1,0:T(8,128)S(1)}, s32[1,1,32,1024]{3,2,1,0:T(8,128)}, u32[]{:S(2)}) copy-start(s32[1,1,32,1024]{3,2,1,0:T(8,128)} %param.7) | copy-start | bytes 393220
  21.6 10.0 %all-to-all-start = ((bf16[2,8,8,512]{3,2,0,1:T(8,128)(2,1)}), bf16[2,8,8,512]{3,2,0,1:T(8,128)(2,1)S(1)}, u32[]{:S(2)}, u32[]{:S(2)}) async-start(bf16[2,8,8,512]{3,2,0,1:T(8,128)(2,1)} %pad_maximum_fusion.7), calls=%async_computation | async-start | bytes 262144 | tf_op jit(solution)/shard_map/all_to_all | solution.py:58
  57.5 8.6 %copy-start.2 = (bf16[54,64]{1,0:T(8,128)(2,1)S(1)}, bf16[54,64]{1,0:T(8,128)(2,1)}, u32[]{:S(2)}) copy-start(bf16[54,64]{1,0:T(8,128)(2,1)} %param.8) | copy-start | bytes 20740
  57.5 8.6 %copy-start.3 = (f32[64]{0:T(128)S(1)}, f32[64]{0:T(128)}, u32[]{:S(2)}) copy-start(f32[64]{0:T(128)} %param.9) | copy-start | bytes 772
  66.1 3.4 %copy-start.4 = (f32[64]{0:T(128)S(1)}, f32[64]{0:T(128)}, u32[]{:S(2)}) copy-start(f32[64]{0:T(128)} %param.11) | copy-start | bytes 772
where the time goes:
time: 135 us
  blocking collectives  40.7 us (30%)
  other arithmetic  32.7 us (24%)
  matrix products  23 us (17%)
  starting transfers between devices  13.3 us (10%)
  waiting for transfers between devices  13.1 us (10%)
  local copies, waits for them, and re-layouts  11.2 us (8%)
    psum x1, blocking collectives, shards(): lax.psum((conv_wsum, conv_bsum, out_wsum, out_bsum), ('sec', 'sp', 'dp'))  40.7 us
    unnamed x26, other arithmetic  24.5 us
    reshape x1, local copies, waits for them, and re-layouts, make_columns(): return stacked.reshape(2 * stacked.shape[0], stacked.shape[2])  8.56 us
    ppermute x2, waiting for transfers between devices, extended(): lax.ppermute(head, axis, [((i + 1) % count, i) for i in range(ends)])  7.66 us
    dot_general x1, matrix products, patch_step(): jnp.einsum('hb,bc->hc', out_weight, residual_low, preferred_element_type=...  7.44 us
    ppermute x2, starting transfers between devices, extended(): lax.ppermute(tail, axis, [(i, (i + 1) % count) for i in range(ends)])  6.17 us
    all_to_all x1, waiting for transfers between devices, relay_features(): lax.all_to_all(block, ('sec', 'sp'), split_axis=1, concat_axis=2, tiled=T...  5.42 us
    dot_general x1, matrix products, patch_step(): jnp.einsum('kc,hc->kh', columns, hidden_low, preferred_element_type=jnp.f...  4.54 us
  transfers between devices with their start and end apart: 5, of which 3 were waited for; matrix products, arithmetic and copies ran while one was open for 0% of the time, Pallas kernels for 0%

commit v1 on v0

v1 whole, which is shorter than its diff:
```python
import functools

import jax
import jax.numpy as jnp
from jax import lax
from jax.experimental import pallas as pl
from jax.experimental.pallas import tpu as pltpu
from jax.sharding import PartitionSpec as P

PZ = 32
TAPS_X = 3
OFFSETS = 9
WINDOW = 8
GROUP = 4
LANES = 512
SLOTS = 4


def rolled(values, step, axis):
    size = values.shape[axis]
    return pltpu.roll(values, (-step) % size, axis)


def neighbour(values, step, axis, inside):
    return jnp.where(inside, rolled(values, step, axis), 0.0)


def window_rows(cells):
    planes, plane = cells.shape
    plane_x = lax.broadcasted_iota(jnp.int32, cells.shape, 0)
    lane = lax.broadcasted_iota(jnp.int32, cells.shape, 1)
    col_z = lane & (PZ - 1)
    has = {
        (0, -1): plane_x > 0,
        (0, 1): plane_x < planes - 1,
        (PZ, -1): lane >= PZ,
        (PZ, 1): lane < plane - PZ,
        (1, -1): col_z > 0,
        (1, 1): col_z < PZ - 1,
    }

    def box(values):
        for stride in (0, PZ, 1):
            axis = 1 if stride else 0
            step = stride or 1
            values = (
                neighbour(values, -step, axis, has[stride, -1])
                + values
                + neighbour(values, step, axis, has[stride, 1])
            )
        return values * (1.0 / 27.0)

    filt = box(cells)
    spread = box(cells * cells) - filt * filt
    channels = (filt, spread)
    place = plane_x & (WINDOW - 1)
    unused = (place == 0) | (place == WINDOW - 1)
    for side, (step, inside) in enumerate(((-2, plane_x >= 2), (2, plane_x < planes - 2))):
        pair = [jnp.where(unused, 1.0, neighbour(v, step, 0, inside)) for v in channels]
        for k in range(planes // WINDOW):
            rows = [v[k * WINDOW : (k + 1) * WINDOW] for v in pair]
            yield 2 * k + side, jnp.concatenate(rows, axis=0).astype(jnp.bfloat16)


def neighbour_rows(offset):
    return slice(offset * 2 * WINDOW, (offset + 1) * 2 * WINDOW)


def spread_window(window_ref, offset):
    both = window_ref[neighbour_rows(OFFSETS // 2), :]
    step_y, step_z = offset // 3 - 1, offset % 3 - 1
    lane = lax.broadcasted_iota(jnp.int32, both.shape, 1)
    row_y, col_z = lane + step_y * PZ, (lane & (PZ - 1)) + step_z
    inside = (row_y >= 0) & (row_y < both.shape[1]) & (col_z >= 0) & (col_z < PZ)
    values = rolled(both, step_y * PZ + step_z, 1)
    window_ref[neighbour_rows(offset), :] = jnp.where(inside, values, jnp.zeros((), both.dtype))


def contract_cells(left, right):
    return lax.dot_general(
        left, right, (((1,), (1,)), ((), ())), preferred_element_type=jnp.float32
    )


def fold_lanes(values):
    parts = [values[:, i : i + 128] for i in range(0, values.shape[1], 128)]
    return functools.reduce(jnp.add, parts)


def inverse(values):
    rough = pltpu.reciprocal(values, approx=True)
    return rough * (2.0 - values * rough)


def train_patch(
    scale, arrived_ref, labels_ref, conv_ref, out_t_ref, out_ref, loss_ref, grads_ref,
    windows, acts, slopes, residuals, hidden_low, conv_acc, out_acc, conv_bias_acc, out_bias_acc,
    sums, picked, losses, turned_ref, loss_sems,
):
    planes, plane = labels_ref.shape
    taps = conv_ref.shape[1]
    hidden, bins = out_ref.shape
    across = plane // LANES
    tiles = planes // GROUP * across
    cells = jnp.concatenate([arrived_ref[s] for s in range(arrived_ref.shape[0])], axis=1)
    for window, both in window_rows(cells):
        windows[window][neighbour_rows(OFFSETS // 2), :] = both
    beside = [offset for offset in range(OFFSETS) if offset != OFFSETS // 2]
    for offset in beside:
        spread_window(windows[0], offset)
    for ref in (conv_acc, out_acc, conv_bias_acc, out_bias_acc):
        ref[...] = jnp.zeros_like(ref)
    for refs in acts:
        for ref in refs:
            ref[hidden:, :] = jnp.ones((ref.shape[0] - hidden, LANES), jnp.bfloat16)
    bin_ids = lax.broadcasted_iota(jnp.int32, (bins, LANES), 0)

    def place(n):
        return n // across, pl.ds(n % across * LANES, LANES)

    def finish_losses(block):
        rows = pl.ds(block * 8, 8)
        losses[rows, :] = jnp.log(sums[rows, :]) - picked[rows, :]
        return pltpu.make_async_copy(losses.at[rows, :], loss_ref.at[rows, :], loss_sems.at[block])

    def dot(left, right):
        return jnp.dot(left, right, preferred_element_type=jnp.float32)

    def convolve(n, q):
        window, lanes = place(n)
        return dot(conv_ref[q * hidden : (q + 1) * hidden, :], windows[window][:, lanes])

    def products(n, slot, q, back, soft, act):
        return (
            dot(out_ref[...], residuals[(slot - 2) % SLOTS][q][...]) if back else None,
            dot(out_t_ref[...], acts[(slot - 1) % SLOTS][q][...]) if soft else None,
            convolve(n, q) if act else None,
        )

    def project_grad(slot):
        slot = (slot - 3) % SLOTS
        return contract_cells(
            jnp.concatenate([ref[:hidden, :] for ref in acts[slot]], axis=1),
            jnp.concatenate([ref[...] for ref in residuals[slot]], axis=1),
        )

    def convolve_grad(n, slot):
        window, lanes = place(n - 3)
        return contract_cells(
            windows[window][:, lanes],
            jnp.concatenate([ref[...] for ref in hidden_low[(slot - 3) % SLOTS]], axis=0),
        )

    def unactivate(slot, q, back):
        slot = (slot - 2) % SLOTS
        hidden_grad = back * slopes[slot][q][...]
        hidden_low[slot][q][...] = hidden_grad.astype(jnp.bfloat16)
        return fold_lanes(hidden_grad)

    def soften(n, slot, q, logits):
        window, lanes = place(n - 1)
        row = pl.ds(window * GROUP + q, 1)
        exp_logits = jnp.exp(logits)
        partition = jnp.sum(exp_logits, axis=0, keepdims=True)
        is_label = bin_ids == labels_ref[row, lanes]
        sums[row, lanes] = partition
        picked[row, lanes] = jnp.sum(jnp.where(is_label, logits, 0.0), axis=0, keepdims=True)
        residual = exp_logits * (scale * inverse(partition)) - jnp.where(is_label, scale, 0.0)
        residuals[(slot - 1) % SLOTS][q][...] = residual.astype(jnp.bfloat16)
        return fold_lanes(residual)

    def activate(slot, q, half):
        tanh = jnp.tanh(half)
        upper = 1.0 + tanh
        act = half * upper
        acts[slot % SLOTS][q][:hidden, :] = act.astype(jnp.bfloat16)
        slopes[slot % SLOTS][q][...] = upper + act * (1.0 - tanh)

    def has(n):
        return 0 <= n < tiles

    def issue(n, q):
        return products(n, n, q, has(n - 2), has(n - 1), has(n))

    def run(count):
        ahead = issue(0, 0)
        copies = []
        share = pl.cdiv(len(beside), across * GROUP)
        for n in range(count):
            conv_bias, out_bias, out_grad, conv_grad = [], [], None, None
            for q in range(GROUP):
                back, logits, half = ahead
                if n // across + 1 < len(windows):
                    first = (n % across * GROUP + q) * share
                    for offset in beside[first : first + share]:
                        spread_window(windows[n // across + 1], offset)
                ahead = issue(n, q + 1) if q + 1 < GROUP else issue(n + 1, 0)
                if q == 0 and has(n - 3):
                    out_grad = project_grad(n)
                if q == 1 and has(n - 3):
                    conv_grad = convolve_grad(n, n)
                if back is not None:
                    conv_bias.append(unactivate(n, q, back))
                if logits is not None:
                    out_bias.append(soften(n, n, q, logits))
                if half is not None:
                    activate(n, q, half)
            if has(n - 3):
                out_acc[...] += out_grad
                conv_acc[...] += conv_grad
            if conv_bias:
                conv_bias_acc[...] += functools.reduce(jnp.add, conv_bias)
            if out_bias:
                out_bias_acc[...] += functools.reduce(jnp.add, out_bias)
            if has(n - 1) and n * GROUP % (8 * across) == 0:
                copies.append(finish_losses(n * GROUP // (8 * across) - 1))
                copies[-1].start()
        return copies

    copies = run(tiles + 3)

    for k in range(turned_ref.shape[0]):
        turned_ref[k] = conv_acc[:, k * 128 : (k + 1) * 128]
    parts = []
    for tap in range(TAPS_X):
        kept = []
        for q in range(GROUP):
            lane = q * hidden % 128
            rows = pl.ds(q + 1 + tap, taps // WINDOW, stride=WINDOW)
            kept.append(turned_ref[q * hidden // 128, rows, :][:, lane : lane + hidden])
        parts.append(functools.reduce(jnp.add, kept))
    parts.append(jnp.sum(jnp.transpose(conv_bias_acc[...]), axis=0, keepdims=True))
    parts.append(jnp.sum(jnp.transpose(out_bias_acc[...]), axis=0, keepdims=True))
    spare = hidden - sum(part.shape[0] for part in parts)
    parts.append(jnp.zeros((spare, hidden), jnp.float32))
    grads_ref[...] = jnp.concatenate([jnp.concatenate(parts, axis=0), out_acc[...]], axis=1)
    for copy in copies:
        copy.wait()


def unpack(total_ref, conv_ref, conv_bias_ref, out_ref, out_bias_ref):
    used, hidden = conv_ref.shape
    conv_ref[...] = total_ref[:used, :hidden]
    conv_bias_ref[...] = total_ref[used : used + 1, :hidden]
    out_ref[...] = total_ref[:, hidden:]
    out_bias_ref[...] = total_ref[used + 1 : used + 2, :hidden]


AXES = ("sec", "sp", "dp")


def factors(size):
    stride = 1
    while stride < size:
        left = size // stride
        radix = next(p for p in range(2, left + 1) if left % p == 0)
        yield stride, radix
        stride *= radix


def moved(place, rounds, steps, sizes):
    for (axis, inner, radix), step in zip(rounds, steps):
        for size in sizes[axis + 1 :]:
            inner *= size
        digit = place // inner % radix
        place += ((digit + step) % radix - digit) * inner
    return place


def summed(value):
    sizes = [lax.axis_size(axis) for axis in AXES]
    total = sizes[0] * sizes[1] * sizes[2]
    rounds = [(axis, *f) for axis in (1, 0, 2) for f in factors(sizes[axis])]
    halvings = [r for r in rounds if r[2] == 2]
    groups = [halvings[:1]] + [halvings[i : i + 2] for i in range(1, len(halvings), 2)]
    groups += [[r] for r in rounds if r[2] != 2]

    def sent(rounds, steps):
        return lax.ppermute(
            value, AXES, [(i, moved(i, rounds, steps, sizes)) for i in range(total)]
        )

    for group in groups:
        if len(group) == 2:
            near, far, last = [sent(group, steps) for steps in ((1, 0), (0, 1), (1, 1))]
            value = (value + near) + (far + last)
        elif group[0][2] == 2:
            value = value + sent(group, (1,))
        else:
            axis, stride, radix = group[0]
            terms = [value] + [sent(group, (k,)) for k in range(1, radix)]
            mine = lax.axis_index(AXES[axis]) // stride % radix
            stacked = jnp.stack(terms + terms)[::-1]
            value = jnp.sum(lax.dynamic_slice_in_dim(stacked, radix - 1 - mine, radix), axis=0)
    return value


def three_terms(bias):
    terms = []
    for _ in range(3):
        term = bias.astype(jnp.bfloat16).astype(jnp.float32)
        terms.append(term)
        bias = bias - term
    return terms


def prepare(*refs):
    given, (banded_ref, out_t_ref, out_half_ref), turned_ref, held, sems = refs[:4], refs[4:7], *refs[7:]
    copies = [pltpu.make_async_copy(g, h, sems.at[k]) for k, (g, h) in enumerate(zip(given, held))]
    for copy in copies:
        copy.start()
    for copy in copies:
        copy.wait()
    conv_ref, conv_bias_ref, out_ref, out_bias_ref = held
    hidden, bins = out_ref.shape
    turned_ref[...] = jnp.zeros_like(turned_ref)
    conv = 0.5 * conv_ref[...].astype(jnp.float32)
    empty = jnp.zeros((2 * OFFSETS, hidden), jnp.float32)
    for q in range(GROUP):
        for tap in range(TAPS_X):
            part = conv[tap * 2 * OFFSETS : (tap + 1) * 2 * OFFSETS]
            pair = [part, empty] if q % 2 == 0 else [empty, part]
            rows = pl.ds(q + 1 + tap, 2 * OFFSETS, stride=WINDOW)
            turned_ref[q // 2, rows, :] += jnp.concatenate(pair, axis=1)
    center = (OFFSETS - 1) * WINDOW
    places = (center, center + WINDOW, center + WINDOW - 1)
    for row, term in zip(places, three_terms(0.5 * conv_bias_ref[...])):
        for k in range(GROUP // 2):
            turned_ref[k, row : row + 1, :] = jnp.concatenate([term, term], axis=1)
    for k in range(GROUP // 2):
        banded_ref[2 * k * hidden : 2 * (k + 1) * hidden, :] = jnp.transpose(turned_ref[k]).astype(
            jnp.bfloat16
        )
    out = out_ref[...].astype(jnp.float32)
    spare = jnp.zeros((out_t_ref.shape[1] - hidden - 3, bins), jnp.float32)
    extended = jnp.concatenate([out] + three_terms(out_bias_ref[...]) + [spare], axis=0)
    out_t_ref[...] = jnp.transpose(extended).astype(jnp.bfloat16)
    out_half_ref[...] = (0.5 * out).astype(jnp.bfloat16)


def prepared_weights(conv_weight, conv_bias, out_weight, out_bias):
    hidden, bins = out_weight.shape
    taps = 2 * OFFSETS * WINDOW
    vmem = pl.BlockSpec(memory_space=pltpu.VMEM)
    given = (conv_weight, conv_bias.reshape(1, hidden), out_weight, out_bias.reshape(1, bins))
    return pl.pallas_call(
        prepare,
        out_shape=(
            jax.ShapeDtypeStruct((GROUP * hidden, taps), jnp.bfloat16),
            jax.ShapeDtypeStruct((bins, hidden + 16), jnp.bfloat16),
            jax.ShapeDtypeStruct((hidden, bins), jnp.bfloat16),
        ),
        in_specs=[pl.BlockSpec(memory_space=pltpu.HBM)] * 4,
        out_specs=(vmem,) * 3,
        scratch_shapes=[
            pltpu.VMEM((GROUP // 2, taps, 2 * hidden), jnp.float32),
            [pltpu.VMEM(g.shape, g.dtype) for g in given],
            pltpu.SemaphoreType.DMA((4,)),
        ],
        compiler_params=pltpu.CompilerParams(vmem_limit_bytes=40 * 1024 * 1024),
        cost_estimate=pl.CostEstimate(flops=1000000, bytes_accessed=1000000, transcendentals=0),
        name="prepare",
    )(*given)


def shards(fraction, labels, conv_weight, conv_bias, out_weight, out_bias):
    sections = lax.axis_size("sec")
    brick = fraction[0]
    arrived = lax.all_to_all(brick, ("sec", "sp"), split_axis=0, concat_axis=1, tiled=True)
    width = arrived.shape[2]
    arrived = arrived.reshape(sections, -1, width)
    patch_labels = labels.reshape(labels.shape[2:])
    planes, plane = patch_labels.shape
    hidden, bins = out_weight.shape
    scale = 1.0 / (lax.axis_size("sec") * lax.axis_size("sp") * lax.axis_size("dp") * planes * plane)
    weights = prepared_weights(conv_weight, conv_bias, out_weight, out_bias)
    taps = weights[0].shape[1]
    vmem = pl.BlockSpec(memory_space=pltpu.VMEM)
    rows = GROUP * hidden
    loss, grads = pl.pallas_call(
        functools.partial(train_patch, scale),
        out_shape=(
            jax.ShapeDtypeStruct((planes, plane), jnp.float32),
            jax.ShapeDtypeStruct((hidden, hidden + bins), jnp.float32),
        ),
        in_specs=[vmem] * 5,
        out_specs=(pl.BlockSpec(memory_space=pl.ANY), vmem),
        scratch_shapes=[
            [pltpu.VMEM((taps, plane), jnp.bfloat16)] * (planes // GROUP),
            [[pltpu.VMEM((weights[1].shape[1], LANES), jnp.bfloat16)] * GROUP] * SLOTS,
            [[pltpu.VMEM((hidden, LANES), jnp.float32)] * GROUP] * SLOTS,
            [[pltpu.VMEM((bins, LANES), jnp.bfloat16)] * GROUP] * SLOTS,
            [[pltpu.VMEM((hidden, LANES), jnp.bfloat16)] * GROUP] * SLOTS,
            pltpu.VMEM((taps, rows), jnp.float32),
            pltpu.VMEM((hidden, bins), jnp.float32),
            pltpu.VMEM((hidden, 128), jnp.float32),
            pltpu.VMEM((bins, 128), jnp.float32),
            pltpu.VMEM((planes, plane), jnp.float32),
            pltpu.VMEM((planes, plane), jnp.float32),
            pltpu.VMEM((planes, plane), jnp.float32),
            pltpu.VMEM((rows // 128, taps, 128), jnp.float32),
            pltpu.SemaphoreType.DMA((planes // 8,)),
        ],
        compiler_params=pltpu.CompilerParams(vmem_limit_bytes=24 * 1024 * 1024),
        name="train_patch",
    )(arrived, patch_labels, *weights)
    shapes = (conv_weight.shape, (1, hidden), out_weight.shape, (1, bins))
    conv_grad, conv_bias_grad, out_grad, out_bias_grad = pl.pallas_call(
        unpack,
        out_shape=tuple(jax.ShapeDtypeStruct(shape, jnp.float32) for shape in shapes),
        in_specs=[vmem],
        out_specs=(vmem,) * 4,
        compiler_params=pltpu.CompilerParams(vmem_limit_bytes=8 * 1024 * 1024),
        name="unpack",
    )(summed(grads))
    return (
        loss.reshape(labels.shape),
        conv_grad,
        conv_bias_grad.reshape(conv_bias.shape),
        out_grad,
        out_bias_grad.reshape(out_bias.shape),
    )


def solution(mesh):
    placed = (P("dp", None, "sp", "sec"), P("dp", ("sec", "sp"), None, None), P(), P(), P(), P())
    return jax.shard_map(
        shards,
        mesh=mesh,
        in_specs=placed,
        out_specs=(P("dp", ("sec", "sp"), None, None), P(), P(), P(), P()),
        check_vma=False,
    )
```

time: 135 us -> 37.9 us (0.28)
  blocking collectives: 40.7 us -> 0 us
  other arithmetic: 32.7 us -> 0.02 us
  matrix products: 23 us -> 0 us
  Pallas kernels: 0 us -> 10.7 us
  local copies, waits for them, and re-layouts: 11.2 us -> 0.65 us
    psum x1 -> x0, blocking collectives: 40.7 us -> none  [shards(): lax.psum((conv_wsum, conv_bsum, out_wsum, out_bsum), ('sec', 'sp', 'dp'))]
    unnamed x26 -> x0, other arithmetic: 24.5 us -> none
    dot_general x5 -> x0, matrix products: 23 us -> none  [the longest x1 7.44 us: patch_step(): jnp.einsum('hb,bc->hc', out_weight, residual_low, preferred_element_type=...]
    pallas_call x0 -> x3, Pallas kernels: none -> 10.7 us  [the longest x1 9.69 us: shards(): pl.pallas_call(functools.partial(train_patch, scale), out_shape=(jax.Shap...]
    reshape x1 -> x0, local copies, waits for them, and re-layouts: 8.56 us -> none  [make_columns(): return stacked.reshape(2 * stacked.shape[0], stacked.shape[2])]
    reduce_sum x1 -> x0, other arithmetic: 4.29 us -> none  [patch_step(): out_bias_grad = jnp.sum(residual, axis=1)]
    another operation x3 -> x0, other arithmetic: 2.5 us -> none  [the longest x1 0.95 us: make_columns(): stacked = jnp.stack(shifted_list)]
    another operation x5 -> x0, local copies, waits for them, and re-layouts: 1.71 us -> none  [the longest x1 1.08 us: shards(): cubic = brick.reshape(patch_total, plane_count, row_width // PZ, PZ)]
  transfers between devices with their start and end apart: 5 -> 8, of which waited for: 3 -> 6; matrix products, arithmetic and copies ran while one was open for 0% -> 0% of each run, Pallas kernels for 0% -> 1%
where the time goes in v1:
time: 37.9 us; the launch traced here: 37.6 us
  starting transfers between devices  13.3 us (35%)
  waiting for transfers between devices  12.2 us (32%)
  Pallas kernels  10.7 us (28%)
  between operations  0.72 us (2%)
  local copies, waits for them, and re-layouts  0.65 us (2%)
    pallas_call x1, Pallas kernels, shards(): pl.pallas_call(functools.partial(train_patch, scale), out_shape=(jax.Shap...  9.69 us
    ppermute x7, starting transfers between devices, sent(): lax.ppermute(value, AXES, [(i, moved(i, rounds, steps, sizes)) for i in r...  8.01 us
    ppermute x7, waiting for transfers between devices, sent(): lax.ppermute(value, AXES, [(i, moved(i, rounds, steps, sizes)) for i in r...  7.68 us
    all_to_all x1, starting transfers between devices, shards(): lax.all_to_all(brick, ('sec', 'sp'), split_axis=0, concat_axis=1, tiled=T...  5.31 us
    all_to_all x1, waiting for transfers between devices, shards(): lax.all_to_all(brick, ('sec', 'sp'), split_axis=0, concat_axis=1, tiled=T...  4.57 us
  transfers between devices with their start and end apart: 8, of which 6 were waited for; matrix products, arithmetic and copies ran while one was open for 0% of the time, Pallas kernels for 1%

profile of v1, /device:TPU:0, one launch (start us, length us, event | category | flops | bytes accessed | tf_op | source)
XLA Modules:
  0.0 37.6 jit_solution(5431075541110624593)
XLA Ops:
  0.6 0.0 copy-start.1
  0.6 0.0 copy-start.2
  0.7 5.3 %all-to-all-start = ((f32[8,8,512]{2,1,0:T(8,128)}), f32[8,8,512]{2,1,0:T(8,128)S(1)}, u32[]{:S(2)}, u32[]{:S(2)}) async-start(f32[8,8,512]{2,1,0:T(8,128)} %bitcast.12), calls=%async_computation | async-start | bytes 262144 | tf_op jit(solution)/shard_map/all_to_all | solution.py:369
  6.0 0.0 copy-start.4
  6.0 0.6 %copy-done.3 = f32[64]{0:T(128)S(1)} copy-done((f32[64]{0:T(128)S(1)}, f32[64]{0:T(128)}, u32[]{:S(2)}) %copy-start.3) | copy-done | bytes 280
  6.6 0.0 copy-done.4
  6.6 0.3 prepare.1
  6.9 4.6 %all-to-all-done = f32[8,8,512]{2,1,0:T(8,128)S(1)} async-done(((f32[8,8,512]{2,1,0:T(8,128)}), f32[8,8,512]{2,1,0:T(8,128)S(1)}, u32[]{:S(2)}, u32[]{:S(2)}) %all-to-all-start) | async-done | bytes 131104 | tf_op jit(solution)/shard_map/all_to_all | solution.py:369
  11.5 9.7 %train_patch.1 = (f32[32,1024]{1,0:T(8,128)}, f32[64,128]{1,0:T(8,128)S(1)}) custom-call(f32[2,32,512]{2,1,0:T(8,128)S(1)} %bitcast.8, s32[32,1024]{1,0:T(8,128)S(1)} %bitcast.9, bf16[256,144]{1,0:T(8,128)(2,1)S(1)} %get-tuple-element.14.conv_ref, bf16[64,80]{1,0:T(8,128)(2,1)S(1)} %get-tuple-element.15.out_t_ref, bf16[64,64]{1,0:T(8,128)(2,1)S(1)} %get-tuple-element.16.out_ref), custom_call_target="tpu_custom_call" | custom-call | tf_op jit(solution)/shard_map/train_patch/pallas_call | solution.py:380
  21.2 0.1 collective-permute-start
  21.3 1.2 %collective-permute-done = f32[64,128]{1,0:T(8,128)S(1)} collective-permute-done((f32[64,128]{1,0:T(8,128)S(1)}, f32[64,128]{1,0:T(8,128)S(1)}, u32[]{:S(2)}, u32[]{:S(2)}) %collective-permute-start) | collective-permute-done | bytes 32800 | tf_op jit(solution)/shard_map/ppermute | solution.py:279
  22.5 0.6 %collective-permute-start.3 = (f32[64,128]{1,0:T(8,128)S(1)}, f32[64,128]{1,0:T(8,128)S(1)}, u32[]{:S(2)}, u32[]{:S(2)}) collective-permute-start(f32[64,128]{1,0:T(8,128)S(1)} %add.21), channel_id=1, source_target_pairs={{0,24},{1,25},{2,26},{3,27},{4,28},{5,29},{6,30},{7,31},{8,16},{9,... | collective-permute-start | bytes 98312 | tf_op jit(solution)/shard_map/ppermute | solution.py:279
  23.1 1.5 %collective-permute-start.2 = (f32[64,128]{1,0:T(8,128)S(1)}, f32[64,128]{1,0:T(8,128)S(1)}, u32[]{:S(2)}, u32[]{:S(2)}) collective-permute-start(f32[64,128]{1,0:T(8,128)S(1)} %add.21), channel_id=1, source_target_pairs={{0,16},{1,17},{2,18},{3,19},{4,20},{5,21},{6,22},{7,23},{8,24},{9,... | collective-permute-start | bytes 98312 | tf_op jit(solution)/shard_map/ppermute | solution.py:279
  24.5 1.5 %collective-permute-start.1 = (f32[64,128]{1,0:T(8,128)S(1)}, f32[64,128]{1,0:T(8,128)S(1)}, u32[]{:S(2)}, u32[]{:S(2)}) collective-permute-start(f32[64,128]{1,0:T(8,128)S(1)} %add.21), channel_id=1, source_target_pairs={{0,8},{1,9},{2,10},{3,11},{4,12},{5,13},{6,14},{7,15},{8,0},{9,1},... | collective-permute-start | bytes 98312 | tf_op jit(solution)/shard_map/ppermute | solution.py:279
  26.0 1.4 %collective-permute-done.3 = f32[64,128]{1,0:T(8,128)S(1)} collective-permute-done((f32[64,128]{1,0:T(8,128)S(1)}, f32[64,128]{1,0:T(8,128)S(1)}, u32[]{:S(2)}, u32[]{:S(2)}) %collective-permute-start.3) | collective-permute-done | bytes 32800 | tf_op jit(solution)/shard_map/ppermute | solution.py:279
  27.4 0.0 collective-permute-done.2
  27.4 1.0 %collective-permute-done.1 = f32[64,128]{1,0:T(8,128)S(1)} collective-permute-done((f32[64,128]{1,0:T(8,128)S(1)}, f32[64,128]{1,0:T(8,128)S(1)}, u32[]{:S(2)}, u32[]{:S(2)}) %collective-permute-start.1) | collective-permute-done | bytes 32800 | tf_op jit(solution)/shard_map/ppermute | solution.py:279
  28.4 3.7 %collective-permute-start.6 = (f32[64,128]{1,0:T(8,128)S(1)}, f32[64,128]{1,0:T(8,128)S(1)}, u32[]{:S(2)}, u32[]{:S(2)}) collective-permute-start(f32[64,128]{1,0:T(8,128)S(1)} %add_add_fusion.1), channel_id=1, source_target_pairs={{0,3},{1,2},{2,1},{3,0},{4,7},{5,6},{6,5},{7,4},{8,11},{9,10},{10,... | collective-permute-start | bytes 98312 | tf_op jit(solution)/shard_map/ppermute | solution.py:279
  32.1 0.0 collective-permute-start.5
  32.1 0.8 %collective-permute-start.4 = (f32[64,128]{1,0:T(8,128)S(1)}, f32[64,128]{1,0:T(8,128)S(1)}, u32[]{:S(2)}, u32[]{:S(2)}) collective-permute-start(f32[64,128]{1,0:T(8,128)S(1)} %add_add_fusion.1), channel_id=1, source_target_pairs={{0,1},{1,0},{2,3},{3,2},{4,5},{5,4},{6,7},{7,6},{8,9},{9,8},{10,11... | collective-permute-start | bytes 98312 | tf_op jit(solution)/shard_map/ppermute | solution.py:279
  32.9 1.3 %collective-permute-done.6 = f32[64,128]{1,0:T(8,128)S(1)} collective-permute-done((f32[64,128]{1,0:T(8,128)S(1)}, f32[64,128]{1,0:T(8,128)S(1)}, u32[]{:S(2)}, u32[]{:S(2)}) %collective-permute-start.6) | collective-permute-done | bytes 32800 | tf_op jit(solution)/shard_map/ppermute | solution.py:279
  34.2 2.7 %collective-permute-done.5 = f32[64,128]{1,0:T(8,128)S(1)} collective-permute-done((f32[64,128]{1,0:T(8,128)S(1)}, f32[64,128]{1,0:T(8,128)S(1)}, u32[]{:S(2)}, u32[]{:S(2)}) %collective-permute-start.5) | collective-permute-done | bytes 32800 | tf_op jit(solution)/shard_map/ppermute | solution.py:279
  36.9 0.0 collective-permute-done.4
  36.9 0.7 %unpack.1 = (f32[54,64]{1,0:T(8,128)}, f32[1,64]{1,0:T(1,128)}, f32[64,64]{1,0:T(8,128)}, f32[1,64]{1,0:T(1,128)}) custom-call(f32[64,128]{1,0:T(8,128)S(1)} %add_add_fusion.total_ref), custom_call_target="tpu_custom_call" | custom-call | tf_op jit(solution)/shard_map/unpack/pallas_call | solution.py:408
  (8 shorter events, 0.0 us)
Async XLA Ops:
  0.6 5.4 %copy-start.1 = (bf16[64,64]{1,0:T(8,128)(2,1)S(1)}, bf16[64,64]{1,0:T(8,128)(2,1)}, u32[]{:S(2)}) copy-start(bf16[64,64]{1,0:T(8,128)(2,1)} %refs_2_.1) | copy-start | bytes 24580
  0.6 5.4 %copy-start.2 = (bf16[54,64]{1,0:T(8,128)(2,1)S(1)}, bf16[54,64]{1,0:T(8,128)(2,1)}, u32[]{:S(2)}) copy-start(bf16[54,64]{1,0:T(8,128)(2,1)} %refs_0_.1) | copy-start | bytes 20740
  0.7 10.9 %copy-start = (s32[1,1,32,1024]{3,2,1,0:T(8,128)S(1)}, s32[1,1,32,1024]{3,2,1,0:T(8,128)}, u32[]{:S(2)}) copy-start(s32[1,1,32,1024]{3,2,1,0:T(8,128)} %param.7) | copy-start | bytes 393220
  0.7 10.8 %all-to-all-start = ((f32[8,8,512]{2,1,0:T(8,128)}), f32[8,8,512]{2,1,0:T(8,128)S(1)}, u32[]{:S(2)}, u32[]{:S(2)}) async-start(f32[8,8,512]{2,1,0:T(8,128)} %bitcast.12), calls=%async_computation | async-start | bytes 262144 | tf_op jit(solution)/shard_map/all_to_all | solution.py:369
  6.0 0.7 %copy-start.3 = (f32[64]{0:T(128)S(1)}, f32[64]{0:T(128)}, u32[]{:S(2)}) copy-start(f32[64]{0:T(128)} %param.9) | copy-start | bytes 772
  6.0 0.7 %copy-start.4 = (f32[64]{0:T(128)S(1)}, f32[64]{0:T(128)}, u32[]{:S(2)}) copy-start(f32[64]{0:T(128)} %param.11) | copy-start | bytes 772
  21.2 1.3 %collective-permute-start = (f32[64,128]{1,0:T(8,128)S(1)}, f32[64,128]{1,0:T(8,128)S(1)}, u32[]{:S(2)}, u32[]{:S(2)}) collective-permute-start(f32[64,128]{1,0:T(8,128)S(1)} %get-tuple-element.18), channel_id=1, source_target_pairs={{0,4},{1,5},{2,6},{3,7},{4,0},{5,1},{6,2},{7,3},{8,12},{9,13},{10,... | collective-permute-start | bytes 98312 | tf_op jit(solution)/shard_map/ppermute | solution.py:279
  22.5 4.9 %collective-permute-start.3 = (f32[64,128]{1,0:T(8,128)S(1)}, f32[64,128]{1,0:T(8,128)S(1)}, u32[]{:S(2)}, u32[]{:S(2)}) collective-permute-start(f32[64,128]{1,0:T(8,128)S(1)} %add.21), channel_id=1, source_target_pairs={{0,24},{1,25},{2,26},{3,27},{4,28},{5,29},{6,30},{7,31},{8,16},{9,... | collective-permute-start | bytes 98312 | tf_op jit(solution)/shard_map/ppermute | solution.py:279
  23.1 4.4 %collective-permute-start.2 = (f32[64,128]{1,0:T(8,128)S(1)}, f32[64,128]{1,0:T(8,128)S(1)}, u32[]{:S(2)}, u32[]{:S(2)}) collective-permute-start(f32[64,128]{1,0:T(8,128)S(1)} %add.21), channel_id=1, source_target_pairs={{0,16},{1,17},{2,18},{3,19},{4,20},{5,21},{6,22},{7,23},{8,24},{9,... | collective-permute-start | bytes 98312 | tf_op jit(solution)/shard_map/ppermute | solution.py:279
  24.5 3.9 %collective-permute-start.1 = (f32[64,128]{1,0:T(8,128)S(1)}, f32[64,128]{1,0:T(8,128)S(1)}, u32[]{:S(2)}, u32[]{:S(2)}) collective-permute-start(f32[64,128]{1,0:T(8,128)S(1)} %add.21), channel_id=1, source_target_pairs={{0,8},{1,9},{2,10},{3,11},{4,12},{5,13},{6,14},{7,15},{8,0},{9,1},... | collective-permute-start | bytes 98312 | tf_op jit(solution)/shard_map/ppermute | solution.py:279
  28.4 5.8 %collective-permute-start.6 = (f32[64,128]{1,0:T(8,128)S(1)}, f32[64,128]{1,0:T(8,128)S(1)}, u32[]{:S(2)}, u32[]{:S(2)}) collective-permute-start(f32[64,128]{1,0:T(8,128)S(1)} %add_add_fusion.1), channel_id=1, source_target_pairs={{0,3},{1,2},{2,1},{3,0},{4,7},{5,6},{6,5},{7,4},{8,11},{9,10},{10,... | collective-permute-start | bytes 98312 | tf_op jit(solution)/shard_map/ppermute | solution.py:279
  32.1 4.8 %collective-permute-start.5 = (f32[64,128]{1,0:T(8,128)S(1)}, f32[64,128]{1,0:T(8,128)S(1)}, u32[]{:S(2)}, u32[]{:S(2)}) collective-permute-start(f32[64,128]{1,0:T(8,128)S(1)} %add_add_fusion.1), channel_id=1, source_target_pairs={{0,2},{1,3},{2,0},{3,1},{4,6},{5,7},{6,4},{7,5},{8,10},{9,11},{10,... | collective-permute-start | bytes 98312 | tf_op jit(solution)/shard_map/ppermute | solution.py:279
  32.1 4.8 %collective-permute-start.4 = (f32[64,128]{1,0:T(8,128)S(1)}, f32[64,128]{1,0:T(8,128)S(1)}, u32[]{:S(2)}, u32[]{:S(2)}) collective-permute-start(f32[64,128]{1,0:T(8,128)S(1)} %add_add_fusion.1), channel_id=1, source_target_pairs={{0,1},{1,0},{2,3},{3,2},{4,5},{5,4},{6,7},{7,6},{8,9},{9,8},{10,11... | collective-permute-start | bytes 98312 | tf_op jit(solution)/shard_map/ppermute | solution.py:279

commit v2 on v1

--- a/solution.py
+++ b/solution.py
@@ -126,9 +126,13 @@
     def dot(left, right):
         return jnp.dot(left, right, preferred_element_type=jnp.float32)
 
+    halves = [None]
+
     def convolve(n, q):
         window, lanes = place(n)
-        return dot(conv_ref[q * hidden : (q + 1) * hidden, :], windows[window][:, lanes])
+        if q == 0:
+            halves[0] = dot(conv_ref[...], windows[window][:, lanes])
+        return halves[0][q * hidden : (q + 1) * hidden]
 
     def products(n, slot, q, back, soft, act):
         return (
@@ -238,12 +242,13 @@
         copy.wait()
 
 
-def unpack(total_ref, conv_ref, conv_bias_ref, out_ref, out_bias_ref):
+def unpack(mine_ref, back_ref, mask_ref, conv_ref, conv_bias_ref, out_ref, out_bias_ref):
     used, hidden = conv_ref.shape
-    conv_ref[...] = total_ref[:used, :hidden]
-    conv_bias_ref[...] = total_ref[used : used + 1, :hidden]
-    out_ref[...] = total_ref[:, hidden:]
-    out_bias_ref[...] = total_ref[used + 1 : used + 2, :hidden]
+    total = jnp.where(mask_ref[...] > 0.0, mine_ref[...], back_ref[...])
+    conv_ref[...] = total[:used, :hidden]
+    conv_bias_ref[...] = total[used : used + 1, :hidden]
+    out_ref[...] = total[:, hidden:]
+    out_bias_ref[...] = total[used + 1 : used + 2, :hidden]
 
 
 AXES = ("sec", "sp", "dp")
@@ -272,14 +277,21 @@
     total = sizes[0] * sizes[1] * sizes[2]
     rounds = [(axis, *f) for axis in (1, 0, 2) for f in factors(sizes[axis])]
     halvings = [r for r in rounds if r[2] == 2]
-    groups = [halvings[:1]] + [halvings[i : i + 2] for i in range(1, len(halvings), 2)]
+    cores, halvings = halvings[:1], halvings[1:]
+    groups = [halvings[i : i + 2] for i in range(0, len(halvings), 2)]
     groups += [[r] for r in rounds if r[2] != 2]
+    near_rounds = groups[0]
 
     def sent(rounds, steps):
-        return lax.ppermute(
-            value, AXES, [(i, moved(i, rounds, steps, sizes)) for i in range(total)]
-        )
-
+        def target(i):
+            if rounds not in (cores, near_rounds) and i // sizes[2] % 2 == 0:
+                turn = (sum(steps) - steps[0]) % len(near_rounds) if len(steps) > 1 else steps[0] % len(near_rounds)
+                return moved(i, [near_rounds[turn]], (1,), sizes)
+            return moved(i, rounds, steps, sizes)
+
+        return lax.ppermute(value, AXES, [(i, target(i)) for i in range(total)])
+
+    value = value + sent(cores, (1,))
     for group in groups:
         if len(group) == 2:
             near, far, last = [sent(group, steps) for steps in ((1, 0), (0, 1), (1, 1))]
@@ -292,7 +304,7 @@
             mine = lax.axis_index(AXES[axis]) // stride % radix
             stacked = jnp.stack(terms + terms)[::-1]
             value = jnp.sum(lax.dynamic_slice_in_dim(stacked, radix - 1 - mine, radix), axis=0)
-    return value
+    return value, sent(cores, (1,))
 
 
 def three_terms(bias):
@@ -376,6 +388,9 @@
     weights = prepared_weights(conv_weight, conv_bias, out_weight, out_bias)
     taps = weights[0].shape[1]
     vmem = pl.BlockSpec(memory_space=pltpu.VMEM)
+    core = (lax.axis_index("sp") & 1).astype(jnp.float32)
+    mask = jnp.broadcast_to(core, (1, hidden + bins))
+    arrived, mask = lax.optimization_barrier((arrived, mask))
     rows = GROUP * hidden
     loss, grads = pl.pallas_call(
         functools.partial(train_patch, scale),
@@ -408,11 +423,11 @@
     conv_grad, conv_bias_grad, out_grad, out_bias_grad = pl.pallas_call(
         unpack,
         out_shape=tuple(jax.ShapeDtypeStruct(shape, jnp.float32) for shape in shapes),
-        in_specs=[vmem],
+        in_specs=[vmem] * 3,
         out_specs=(vmem,) * 4,
         compiler_params=pltpu.CompilerParams(vmem_limit_bytes=8 * 1024 * 1024),
         name="unpack",
-    )(summed(grads))
+    )(*summed(grads), mask)
     return (
         loss.reshape(labels.shape),
         conv_grad,

time: 37.9 us -> 36.5 us (0.963)
  starting transfers between devices: 13.3 us -> 12.5 us
  waiting for transfers between devices: 12.2 us -> 11.8 us
    ppermute x7 -> x8, starting transfers between devices: 8.01 us -> 7.19 us  [sent(): return lax.ppermute(value, AXES, [(i, target(i)) for i in range(total)])]
    ppermute x7 -> x8, waiting for transfers between devices: 7.68 us -> 7.29 us  [sent(): return lax.ppermute(value, AXES, [(i, target(i)) for i in range(total)])]
  transfers between devices with their start and end apart: 8 -> 9, of which waited for: 6 -> 8; matrix products, arithmetic and copies ran while one was open for 0% -> 0% of each run, Pallas kernels for 1% -> 1%
where the time goes in v2:
time: 36.5 us; the launch traced here: 36.1 us
  starting transfers between devices  12.5 us (34%)
  waiting for transfers between devices  11.8 us (32%)
  Pallas kernels  10.4 us (28%)
  between operations  0.73 us (2%)
  local copies, waits for them, and re-layouts  0.69 us (2%)
    pallas_call x1, Pallas kernels, shards(): pl.pallas_call(functools.partial(train_patch, scale), out_shape=(jax.Shap...  9.38 us
    ppermute x8, waiting for transfers between devices, sent(): return lax.ppermute(value, AXES, [(i, target(i)) for i in range(total)])  7.29 us
    ppermute x8, starting transfers between devices, sent(): return lax.ppermute(value, AXES, [(i, target(i)) for i in range(total)])  7.19 us
    all_to_all x1, starting transfers between devices, shards(): lax.all_to_all(brick, ('sec', 'sp'), split_axis=0, concat_axis=1, tiled=T...  5.31 us
    all_to_all x1, waiting for transfers between devices, shards(): lax.all_to_all(brick, ('sec', 'sp'), split_axis=0, concat_axis=1, tiled=T...  4.52 us
  transfers between devices with their start and end apart: 9, of which 8 were waited for; matrix products, arithmetic and copies ran while one was open for 0% of the time, Pallas kernels for 1%

profile of v2, /device:TPU:0, one launch (start us, length us, event | category | flops | bytes accessed | tf_op | source)
XLA Modules:
  0.0 36.1 jit_solution(12692511709791272242)
XLA Ops:
  0.7 5.3 %all-to-all-start = ((f32[8,8,512]{2,1,0:T(8,128)}), f32[8,8,512]{2,1,0:T(8,128)S(1)}, u32[]{:S(2)}, u32[]{:S(2)}) async-start(f32[8,8,512]{2,1,0:T(8,128)} %bitcast.12), calls=%async_computation | async-start | bytes 262144 | tf_op jit(solution)/shard_map/all_to_all | solution.py:381
  6.0 0.0 copy-start.3
  6.0 0.0 copy-start.4
  6.0 0.7 %copy-done.2 = bf16[54,64]{1,0:T(8,128)(2,1)S(1)} copy-done((bf16[54,64]{1,0:T(8,128)(2,1)S(1)}, bf16[54,64]{1,0:T(8,128)(2,1)}, u32[]{:S(2)}) %copy-start.2) | copy-done | bytes 6936
  6.7 0.3 prepare.1
  7.0 4.5 %all-to-all-done = f32[8,8,512]{2,1,0:T(8,128)S(1)} async-done(((f32[8,8,512]{2,1,0:T(8,128)}), f32[8,8,512]{2,1,0:T(8,128)S(1)}, u32[]{:S(2)}, u32[]{:S(2)}) %all-to-all-start) | async-done | bytes 131104 | tf_op jit(solution)/shard_map/all_to_all | solution.py:381
  11.5 9.4 %train_patch.1 = (f32[32,1024]{1,0:T(8,128)}, f32[64,128]{1,0:T(8,128)S(1)}) custom-call(f32[2,32,512]{2,1,0:T(8,128)S(1)} %bitcast.8, s32[32,1024]{1,0:T(8,128)S(1)} %bitcast.9, bf16[256,144]{1,0:T(8,128)(2,1)S(1)} %get-tuple-element.17.conv_ref, bf16[64,80]{1,0:T(8,128)(2,1)S(1)} %get-tuple-element.18.out_t_ref, bf16[64,64]{1,0:T(8,128)(2,1)S(1)} %get-tuple-element.19.out_ref), custom_call_target="tpu_custom_call" | custom-call | tf_op jit(solution)/shard_map/train_patch/pallas_call | solution.py:395
  20.9 0.1 collective-permute-start
  21.0 1.2 %collective-permute-done = f32[64,128]{1,0:T(8,128)S(1)} collective-permute-done((f32[64,128]{1,0:T(8,128)S(1)}, f32[64,128]{1,0:T(8,128)S(1)}, u32[]{:S(2)}, u32[]{:S(2)}) %collective-permute-start) | collective-permute-done | bytes 32800 | tf_op jit(solution)/shard_map/ppermute | solution.py:292
  22.2 0.6 %collective-permute-start.3 = (f32[64,128]{1,0:T(8,128)S(1)}, f32[64,128]{1,0:T(8,128)S(1)}, u32[]{:S(2)}, u32[]{:S(2)}) collective-permute-start(f32[64,128]{1,0:T(8,128)S(1)} %add.21), channel_id=1, source_target_pairs={{0,24},{1,25},{2,26},{3,27},{4,28},{5,29},{6,30},{7,31},{8,16},{9,... | collective-permute-start | bytes 98312 | tf_op jit(solution)/shard_map/ppermute | solution.py:292
  22.7 1.5 %collective-permute-start.2 = (f32[64,128]{1,0:T(8,128)S(1)}, f32[64,128]{1,0:T(8,128)S(1)}, u32[]{:S(2)}, u32[]{:S(2)}) collective-permute-start(f32[64,128]{1,0:T(8,128)S(1)} %add.21), channel_id=1, source_target_pairs={{0,16},{1,17},{2,18},{3,19},{4,20},{5,21},{6,22},{7,23},{8,24},{9,... | collective-permute-start | bytes 98312 | tf_op jit(solution)/shard_map/ppermute | solution.py:292
  24.2 1.5 %collective-permute-start.1 = (f32[64,128]{1,0:T(8,128)S(1)}, f32[64,128]{1,0:T(8,128)S(1)}, u32[]{:S(2)}, u32[]{:S(2)}) collective-permute-start(f32[64,128]{1,0:T(8,128)S(1)} %add.21), channel_id=1, source_target_pairs={{0,8},{1,9},{2,10},{3,11},{4,12},{5,13},{6,14},{7,15},{8,0},{9,1},... | collective-permute-start | bytes 98312 | tf_op jit(solution)/shard_map/ppermute | solution.py:292
  25.7 1.4 %collective-permute-done.3 = f32[64,128]{1,0:T(8,128)S(1)} collective-permute-done((f32[64,128]{1,0:T(8,128)S(1)}, f32[64,128]{1,0:T(8,128)S(1)}, u32[]{:S(2)}, u32[]{:S(2)}) %collective-permute-start.3) | collective-permute-done | bytes 32800 | tf_op jit(solution)/shard_map/ppermute | solution.py:292
  27.1 0.0 collective-permute-done.2
  27.1 1.0 %collective-permute-done.1 = f32[64,128]{1,0:T(8,128)S(1)} collective-permute-done((f32[64,128]{1,0:T(8,128)S(1)}, f32[64,128]{1,0:T(8,128)S(1)}, u32[]{:S(2)}, u32[]{:S(2)}) %collective-permute-start.1) | collective-permute-done | bytes 32800 | tf_op jit(solution)/shard_map/ppermute | solution.py:292
  28.1 0.6 %collective-permute-start.6 = (f32[64,128]{1,0:T(8,128)S(1)}, f32[64,128]{1,0:T(8,128)S(1)}, u32[]{:S(2)}, u32[]{:S(2)}) collective-permute-start(f32[64,128]{1,0:T(8,128)S(1)} %add_add_fusion.1), channel_id=1, source_target_pairs={{0,16},{1,17},{2,18},{3,19},{4,7},{5,6},{6,5},{7,4},{8,24},{9,25},... | collective-permute-start | bytes 98312 | tf_op jit(solution)/shard_map/ppermute | solution.py:292
  28.8 1.5 %collective-permute-start.5 = (f32[64,128]{1,0:T(8,128)S(1)}, f32[64,128]{1,0:T(8,128)S(1)}, u32[]{:S(2)}, u32[]{:S(2)}) collective-permute-start(f32[64,128]{1,0:T(8,128)S(1)} %add_add_fusion.1), channel_id=1, source_target_pairs={{0,16},{1,17},{2,18},{3,19},{4,6},{5,7},{6,4},{7,5},{8,24},{9,25},... | collective-permute-start | bytes 98312 | tf_op jit(solution)/shard_map/ppermute | solution.py:292
  30.2 1.5 %collective-permute-start.4 = (f32[64,128]{1,0:T(8,128)S(1)}, f32[64,128]{1,0:T(8,128)S(1)}, u32[]{:S(2)}, u32[]{:S(2)}) collective-permute-start(f32[64,128]{1,0:T(8,128)S(1)} %add_add_fusion.1), channel_id=1, source_target_pairs={{0,8},{1,9},{2,10},{3,11},{4,5},{5,4},{6,7},{7,6},{8,0},{9,1},{10,... | collective-permute-start | bytes 98312 | tf_op jit(solution)/shard_map/ppermute | solution.py:292
  31.7 0.4 %collective-permute-done.6 = f32[64,128]{1,0:T(8,128)S(1)} collective-permute-done((f32[64,128]{1,0:T(8,128)S(1)}, f32[64,128]{1,0:T(8,128)S(1)}, u32[]{:S(2)}, u32[]{:S(2)}) %collective-permute-start.6) | collective-permute-done | bytes 32800 | tf_op jit(solution)/shard_map/ppermute | solution.py:292
  32.1 0.6 %collective-permute-done.5 = f32[64,128]{1,0:T(8,128)S(1)} collective-permute-done((f32[64,128]{1,0:T(8,128)S(1)}, f32[64,128]{1,0:T(8,128)S(1)}, u32[]{:S(2)}, u32[]{:S(2)}) %collective-permute-start.5) | collective-permute-done | bytes 32800 | tf_op jit(solution)/shard_map/ppermute | solution.py:292
  32.7 1.5 %collective-permute-done.4 = f32[64,128]{1,0:T(8,128)S(1)} collective-permute-done((f32[64,128]{1,0:T(8,128)S(1)}, f32[64,128]{1,0:T(8,128)S(1)}, u32[]{:S(2)}, u32[]{:S(2)}) %collective-permute-start.4) | collective-permute-done | bytes 32800 | tf_op jit(solution)/shard_map/ppermute | solution.py:292
  34.1 0.1 collective-permute-start.7
  34.2 1.2 %collective-permute-done.7.back_ref = f32[64,128]{1,0:T(8,128)S(1)} collective-permute-done((f32[64,128]{1,0:T(8,128)S(1)}, f32[64,128]{1,0:T(8,128)S(1)}, u32[]{:S(2)}, u32[]{:S(2)}) %collective-permute-start.7) | collective-permute-done | bytes 32800 | tf_op jit(solution)/shard_map/ppermute | solution.py:292
  35.4 0.7 %unpack.1 = (f32[54,64]{1,0:T(8,128)}, f32[1,64]{1,0:T(1,128)}, f32[64,64]{1,0:T(8,128)}, f32[1,64]{1,0:T(1,128)}) custom-call(f32[64,128]{1,0:T(8,128)S(1)} %add_add_fusion.mine_ref, f32[64,128]{1,0:T(8,128)S(1)} %collective-permute-done.7.back_ref, f32[1,128]{1,0:T(1,128)S(1)} %broadcast_in_dim.3.mask_ref), custom_call_target="tpu_custom_call" | custom-call | tf_op jit(solution)/shard_map/unpack/pallas_call | solution.py:423
  (11 shorter events, 0.0 us)
Async XLA Ops:
  0.6 5.4 %copy-start.1 = (bf16[64,64]{1,0:T(8,128)(2,1)S(1)}, bf16[64,64]{1,0:T(8,128)(2,1)}, u32[]{:S(2)}) copy-start(bf16[64,64]{1,0:T(8,128)(2,1)} %refs_2_.1) | copy-start | bytes 24580
  0.6 10.9 %copy-start = (s32[1,1,32,1024]{3,2,1,0:T(8,128)S(1)}, s32[1,1,32,1024]{3,2,1,0:T(8,128)}, u32[]{:S(2)}) copy-start(s32[1,1,32,1024]{3,2,1,0:T(8,128)} %param.7) | copy-start | bytes 393220
  0.7 10.8 %all-to-all-start = ((f32[8,8,512]{2,1,0:T(8,128)}), f32[8,8,512]{2,1,0:T(8,128)S(1)}, u32[]{:S(2)}, u32[]{:S(2)}) async-start(f32[8,8,512]{2,1,0:T(8,128)} %bitcast.12), calls=%async_computation | async-start | bytes 262144 | tf_op jit(solution)/shard_map/all_to_all | solution.py:381
  6.0 0.7 %copy-start.2 = (bf16[54,64]{1,0:T(8,128)(2,1)S(1)}, bf16[54,64]{1,0:T(8,128)(2,1)}, u32[]{:S(2)}) copy-start(bf16[54,64]{1,0:T(8,128)(2,1)} %refs_0_.1) | copy-start | bytes 20740
  6.0 0.7 %copy-start.3 = (f32[64]{0:T(128)S(1)}, f32[64]{0:T(128)}, u32[]{:S(2)}) copy-start(f32[64]{0:T(128)} %param.9) | copy-start | bytes 772
  6.0 0.7 %copy-start.4 = (f32[64]{0:T(128)S(1)}, f32[64]{0:T(128)}, u32[]{:S(2)}) copy-start(f32[64]{0:T(128)} %param.11) | copy-start | bytes 772
  20.9 1.3 %collective-permute-start = (f32[64,128]{1,0:T(8,128)S(1)}, f32[64,128]{1,0:T(8,128)S(1)}, u32[]{:S(2)}, u32[]{:S(2)}) collective-permute-start(f32[64,128]{1,0:T(8,128)S(1)} %get-tuple-element.21), channel_id=1, source_target_pairs={{0,4},{1,5},{2,6},{3,7},{4,0},{5,1},{6,2},{7,3},{8,12},{9,13},{10,... | collective-permute-start | bytes 98312 | tf_op jit(solution)/shard_map/ppermute | solution.py:292
  22.2 4.9 %collective-permute-start.3 = (f32[64,128]{1,0:T(8,128)S(1)}, f32[64,128]{1,0:T(8,128)S(1)}, u32[]{:S(2)}, u32[]{:S(2)}) collective-permute-start(f32[64,128]{1,0:T(8,128)S(1)} %add.21), channel_id=1, source_target_pairs={{0,24},{1,25},{2,26},{3,27},{4,28},{5,29},{6,30},{7,31},{8,16},{9,... | collective-permute-start | bytes 98312 | tf_op jit(solution)/shard_map/ppermute | solution.py:292
  22.7 4.4 %collective-permute-start.2 = (f32[64,128]{1,0:T(8,128)S(1)}, f32[64,128]{1,0:T(8,128)S(1)}, u32[]{:S(2)}, u32[]{:S(2)}) collective-permute-start(f32[64,128]{1,0:T(8,128)S(1)} %add.21), channel_id=1, source_target_pairs={{0,16},{1,17},{2,18},{3,19},{4,20},{5,21},{6,22},{7,23},{8,24},{9,... | collective-permute-start | bytes 98312 | tf_op jit(solution)/shard_map/ppermute | solution.py:292
  24.2 3.9 %collective-permute-start.1 = (f32[64,128]{1,0:T(8,128)S(1)}, f32[64,128]{1,0:T(8,128)S(1)}, u32[]{:S(2)}, u32[]{:S(2)}) collective-permute-start(f32[64,128]{1,0:T(8,128)S(1)} %add.21), channel_id=1, source_target_pairs={{0,8},{1,9},{2,10},{3,11},{4,12},{5,13},{6,14},{7,15},{8,0},{9,1},... | collective-permute-start | bytes 98312 | tf_op jit(solution)/shard_map/ppermute | solution.py:292
  28.1 4.0 %collective-permute-start.6 = (f32[64,128]{1,0:T(8,128)S(1)}, f32[64,128]{1,0:T(8,128)S(1)}, u32[]{:S(2)}, u32[]{:S(2)}) collective-permute-start(f32[64,128]{1,0:T(8,128)S(1)} %add_add_fusion.1), channel_id=1, source_target_pairs={{0,16},{1,17},{2,18},{3,19},{4,7},{5,6},{6,5},{7,4},{8,24},{9,25},... | collective-permute-start | bytes 98312 | tf_op jit(solution)/shard_map/ppermute | solution.py:292
  28.8 3.9 %collective-permute-start.5 = (f32[64,128]{1,0:T(8,128)S(1)}, f32[64,128]{1,0:T(8,128)S(1)}, u32[]{:S(2)}, u32[]{:S(2)}) collective-permute-start(f32[64,128]{1,0:T(8,128)S(1)} %add_add_fusion.1), channel_id=1, source_target_pairs={{0,16},{1,17},{2,18},{3,19},{4,6},{5,7},{6,4},{7,5},{8,24},{9,25},... | collective-permute-start | bytes 98312 | tf_op jit(solution)/shard_map/ppermute | solution.py:292
  30.2 3.9 %collective-permute-start.4 = (f32[64,128]{1,0:T(8,128)S(1)}, f32[64,128]{1,0:T(8,128)S(1)}, u32[]{:S(2)}, u32[]{:S(2)}) collective-permute-start(f32[64,128]{1,0:T(8,128)S(1)} %add_add_fusion.1), channel_id=1, source_target_pairs={{0,8},{1,9},{2,10},{3,11},{4,5},{5,4},{6,7},{7,6},{8,0},{9,1},{10,... | collective-permute-start | bytes 98312 | tf_op jit(solution)/shard_map/ppermute | solution.py:292
  34.1 1.3 %collective-permute-start.7 = (f32[64,128]{1,0:T(8,128)S(1)}, f32[64,128]{1,0:T(8,128)S(1)}, u32[]{:S(2)}, u32[]{:S(2)}) collective-permute-start(f32[64,128]{1,0:T(8,128)S(1)} %add_add_fusion.mine_ref), channel_id=1, source_target_pairs={{0,4},{1,5},{2,6},{3,7},{4,0},{5,1},{6,2},{7,3},{8,12},{9,13},{10,... | collective-permute-start | bytes 98312 | tf_op jit(solution)/shard_map/ppermute | solution.py:292

commit v3 on v2

--- a/solution.py
+++ b/solution.py
@@ -242,9 +242,9 @@
         copy.wait()
 
 
-def unpack(mine_ref, back_ref, mask_ref, conv_ref, conv_bias_ref, out_ref, out_bias_ref):
+def unpack(mine_ref, other_ref, conv_ref, conv_bias_ref, out_ref, out_bias_ref):
     used, hidden = conv_ref.shape
-    total = jnp.where(mask_ref[...] > 0.0, mine_ref[...], back_ref[...])
+    total = mine_ref[...] + other_ref[...]
     conv_ref[...] = total[:used, :hidden]
     conv_bias_ref[...] = total[used : used + 1, :hidden]
     out_ref[...] = total[:, hidden:]
@@ -272,39 +272,44 @@
     return place
 
 
-def summed(value):
+def summed(value, mask):
     sizes = [lax.axis_size(axis) for axis in AXES]
     total = sizes[0] * sizes[1] * sizes[2]
     rounds = [(axis, *f) for axis in (1, 0, 2) for f in factors(sizes[axis])]
     halvings = [r for r in rounds if r[2] == 2]
     cores, halvings = halvings[:1], halvings[1:]
-    groups = [halvings[i : i + 2] for i in range(0, len(halvings), 2)]
-    groups += [[r] for r in rounds if r[2] != 2]
-    near_rounds = groups[0]
-
-    def sent(rounds, steps):
-        def target(i):
-            if rounds not in (cores, near_rounds) and i // sizes[2] % 2 == 0:
-                turn = (sum(steps) - steps[0]) % len(near_rounds) if len(steps) > 1 else steps[0] % len(near_rounds)
-                return moved(i, [near_rounds[turn]], (1,), sizes)
-            return moved(i, rounds, steps, sizes)
-
-        return lax.ppermute(value, AXES, [(i, target(i)) for i in range(total)])
-
-    value = value + sent(cores, (1,))
+    near = halvings[:1]
+    groups = [[r] for r in rounds if r[2] != 2] + [halvings[-1:]] * (len(halvings) % 2)
+    groups += [halvings[i : i + 2] for i in range(0, len(halvings) - 1, 2)]
+
+    def sent(value, even, odd):
+        return lax.ppermute(
+            value,
+            AXES,
+            [(i, moved(i, *(odd if i // sizes[2] % 2 else even), sizes)) for i in range(total)],
+        )
+
+    def alike(value, rounds, steps):
+        return sent(value, (rounds, steps), (rounds, steps))
+
+    parts = value, alike(value, cores, (1,))
     for group in groups:
+        value = parts[0] + parts[1]
         if len(group) == 2:
-            near, far, last = [sent(group, steps) for steps in ((1, 0), (0, 1), (1, 1))]
-            value = (value + near) + (far + last)
+            first = sent(value, (group, (1, 0)), (group, (0, 1)))
+            second = sent(value, (near, (1,)), (group, (1, 1)))
+            part = first + jnp.where(mask > 0.0, second, value)
+            parts = part, alike(part, cores, (1,))
         elif group[0][2] == 2:
-            value = value + sent(group, (1,))
+            parts = value, alike(value, group, (1,))
         else:
             axis, stride, radix = group[0]
-            terms = [value] + [sent(group, (k,)) for k in range(1, radix)]
+            terms = [value] + [alike(value, group, (k,)) for k in range(1, radix)]
             mine = lax.axis_index(AXES[axis]) // stride % radix
             stacked = jnp.stack(terms + terms)[::-1]
-            value = jnp.sum(lax.dynamic_slice_in_dim(stacked, radix - 1 - mine, radix), axis=0)
-    return value, sent(cores, (1,))
+            ordered = lax.dynamic_slice_in_dim(stacked, radix - 1 - mine, radix)
+            parts = ordered[0], jnp.sum(ordered[1:], axis=0)
+    return parts
 
 
 def three_terms(bias):
@@ -389,7 +394,7 @@
     taps = weights[0].shape[1]
     vmem = pl.BlockSpec(memory_space=pltpu.VMEM)
     core = (lax.axis_index("sp") & 1).astype(jnp.float32)
-    mask = jnp.broadcast_to(core, (1, hidden + bins))
+    mask = jnp.broadcast_to(core, (hidden, hidden + bins))
     arrived, mask = lax.optimization_barrier((arrived, mask))
     rows = GROUP * hidden
     loss, grads = pl.pallas_call(
@@ -423,11 +428,11 @@
     conv_grad, conv_bias_grad, out_grad, out_bias_grad = pl.pallas_call(
         unpack,
         out_shape=tuple(jax.ShapeDtypeStruct(shape, jnp.float32) for shape in shapes),
-        in_specs=[vmem] * 3,
+        in_specs=[vmem] * 2,
         out_specs=(vmem,) * 4,
         compiler_params=pltpu.CompilerParams(vmem_limit_bytes=8 * 1024 * 1024),
         name="unpack",
-    )(*summed(grads), mask)
+    )(*summed(grads, mask))
     return (
         loss.reshape(labels.shape),
         conv_grad,

time: 36.5 us -> 37.1 us (1.016)
  waiting for transfers between devices: 11.8 us -> 12.6 us
    ppermute x8 -> x7, waiting for transfers between devices: 7.29 us -> 8.04 us  [sent(): lax.ppermute(value, AXES, [(i, moved(i, *(odd if i // sizes[2] % 2 else e...]
    ppermute x8 -> x7, starting transfers between devices: 7.19 us -> 7.05 us  [sent(): lax.ppermute(value, AXES, [(i, moved(i, *(odd if i // sizes[2] % 2 else e...]
  transfers between devices with their start and end apart: 9 -> 8, of which waited for: 8 -> 8; matrix products, arithmetic and copies ran while one was open for 0% -> 0% of each run, Pallas kernels for 1% -> 1%
where the time goes in v3:
time: 37.1 us; the launch traced here: 36.7 us
  waiting for transfers between devices  12.6 us (34%)
  starting transfers between devices  12.4 us (33%)
  Pallas kernels  10.4 us (28%)
  between operations  0.73 us (2%)
  local copies, waits for them, and re-layouts  0.69 us (2%)
    pallas_call x1, Pallas kernels, shards(): pl.pallas_call(functools.partial(train_patch, scale), out_shape=(jax.Shap...  9.38 us
    ppermute x7, waiting for transfers between devices, sent(): lax.ppermute(value, AXES, [(i, moved(i, *(odd if i // sizes[2] % 2 else e...  8.04 us
    ppermute x7, starting transfers between devices, sent(): lax.ppermute(value, AXES, [(i, moved(i, *(odd if i // sizes[2] % 2 else e...  7.05 us
    all_to_all x1, starting transfers between devices, shards(): lax.all_to_all(brick, ('sec', 'sp'), split_axis=0, concat_axis=1, tiled=T...  5.31 us
    all_to_all x1, waiting for transfers between devices, shards(): lax.all_to_all(brick, ('sec', 'sp'), split_axis=0, concat_axis=1, tiled=T...  4.52 us
  transfers between devices with their start and end apart: 8, of which 8 were waited for; matrix products, arithmetic and copies ran while one was open for 0% of the time, Pallas kernels for 1%

profile of v3, /device:TPU:0, one launch (start us, length us, event | category | flops | bytes accessed | tf_op | source)
XLA Modules:
  0.0 36.7 jit_solution(8366370386950588401)
XLA Ops:
  0.6 0.0 copy-start.1
  0.6 0.0 copy-start
  0.7 5.3 %all-to-all-start = ((f32[8,8,512]{2,1,0:T(8,128)}), f32[8,8,512]{2,1,0:T(8,128)S(1)}, u32[]{:S(2)}, u32[]{:S(2)}) async-start(f32[8,8,512]{2,1,0:T(8,128)} %bitcast.12), calls=%async_computation | async-start | bytes 262144 | tf_op jit(solution)/shard_map/all_to_all | solution.py:386
  6.0 0.0 copy-start.3
  6.0 0.0 copy-start.4
  6.0 0.7 %copy-done.2 = bf16[54,64]{1,0:T(8,128)(2,1)S(1)} copy-done((bf16[54,64]{1,0:T(8,128)(2,1)S(1)}, bf16[54,64]{1,0:T(8,128)(2,1)}, u32[]{:S(2)}) %copy-start.2) | copy-done | bytes 6936
  6.7 0.3 prepare.1
  7.0 4.5 %all-to-all-done = f32[8,8,512]{2,1,0:T(8,128)S(1)} async-done(((f32[8,8,512]{2,1,0:T(8,128)}), f32[8,8,512]{2,1,0:T(8,128)S(1)}, u32[]{:S(2)}, u32[]{:S(2)}) %all-to-all-start) | async-done | bytes 131104 | tf_op jit(solution)/shard_map/all_to_all | solution.py:386
  11.5 9.4 %train_patch.1 = (f32[32,1024]{1,0:T(8,128)}, f32[64,128]{1,0:T(8,128)S(1)}) custom-call(f32[2,32,512]{2,1,0:T(8,128)S(1)} %bitcast.8, s32[32,1024]{1,0:T(8,128)S(1)} %bitcast.9, bf16[256,144]{1,0:T(8,128)(2,1)S(1)} %get-tuple-element.17.conv_ref, bf16[64,80]{1,0:T(8,128)(2,1)S(1)} %get-tuple-element.18.out_t_ref, bf16[64,64]{1,0:T(8,128)(2,1)S(1)} %get-tuple-element.19.out_ref), custom_call_target="tpu_custom_call" | custom-call | tf_op jit(solution)/shard_map/train_patch/pallas_call | solution.py:400
  20.9 0.1 collective-permute-start
  21.0 1.2 %collective-permute-done = f32[64,128]{1,0:T(8,128)S(1)} collective-permute-done((f32[64,128]{1,0:T(8,128)S(1)}, f32[64,128]{1,0:T(8,128)S(1)}, u32[]{:S(2)}, u32[]{:S(2)}) %collective-permute-start) | collective-permute-done | bytes 32800 | tf_op jit(solution)/shard_map/ppermute | solution.py:286
  22.2 0.6 %collective-permute-start.2 = (f32[64,128]{1,0:T(8,128)S(1)}, f32[64,128]{1,0:T(8,128)S(1)}, u32[]{:S(2)}, u32[]{:S(2)}) collective-permute-start(f32[64,128]{1,0:T(8,128)S(1)} %add.12), channel_id=1, source_target_pairs={{0,8},{1,9},{2,10},{3,11},{4,28},{5,29},{6,30},{7,31},{8,0},{9,1},... | collective-permute-start | bytes 98312 | tf_op jit(solution)/shard_map/ppermute | solution.py:286
  22.7 1.5 %collective-permute-start.1 = (f32[64,128]{1,0:T(8,128)S(1)}, f32[64,128]{1,0:T(8,128)S(1)}, u32[]{:S(2)}, u32[]{:S(2)}) collective-permute-start(f32[64,128]{1,0:T(8,128)S(1)} %add.12), channel_id=1, source_target_pairs={{0,8},{1,9},{2,10},{3,11},{4,20},{5,21},{6,22},{7,23},{8,0},{9,1},... | collective-permute-start | bytes 98312 | tf_op jit(solution)/shard_map/ppermute | solution.py:286
  24.2 1.9 %collective-permute-done.2 = f32[64,128]{1,0:T(8,128)S(1)} collective-permute-done((f32[64,128]{1,0:T(8,128)S(1)}, f32[64,128]{1,0:T(8,128)S(1)}, u32[]{:S(2)}, u32[]{:S(2)}) %collective-permute-start.2) | collective-permute-done | bytes 32800 | tf_op jit(solution)/shard_map/ppermute | solution.py:286
  26.1 0.6 %collective-permute-done.1 = f32[64,128]{1,0:T(8,128)S(1)} collective-permute-done((f32[64,128]{1,0:T(8,128)S(1)}, f32[64,128]{1,0:T(8,128)S(1)}, u32[]{:S(2)}, u32[]{:S(2)}) %collective-permute-start.1) | collective-permute-done | bytes 32800 | tf_op jit(solution)/shard_map/ppermute | solution.py:286
  26.7 0.1 collective-permute-start.3
  26.7 1.2 %collective-permute-done.3 = f32[64,128]{1,0:T(8,128)S(1)} collective-permute-done((f32[64,128]{1,0:T(8,128)S(1)}, f32[64,128]{1,0:T(8,128)S(1)}, u32[]{:S(2)}, u32[]{:S(2)}) %collective-permute-start.3) | collective-permute-done | bytes 32800 | tf_op jit(solution)/shard_map/ppermute | solution.py:286
  27.9 1.5 %collective-permute-start.5 = (f32[64,128]{1,0:T(8,128)S(1)}, f32[64,128]{1,0:T(8,128)S(1)}, u32[]{:S(2)}, u32[]{:S(2)}) collective-permute-start(f32[64,128]{1,0:T(8,128)S(1)} %add.14), channel_id=1, source_target_pairs={{0,8},{1,9},{2,10},{3,11},{4,7},{5,6},{6,5},{7,4},{8,0},{9,1},{10,... | collective-permute-start | bytes 98312 | tf_op jit(solution)/shard_map/ppermute | solution.py:286
  29.4 1.6 %collective-permute-start.4 = (f32[64,128]{1,0:T(8,128)S(1)}, f32[64,128]{1,0:T(8,128)S(1)}, u32[]{:S(2)}, u32[]{:S(2)}) collective-permute-start(f32[64,128]{1,0:T(8,128)S(1)} %add.14), channel_id=1, source_target_pairs={{0,1},{1,0},{2,3},{3,2},{4,6},{5,7},{6,4},{7,5},{8,9},{9,8},{10,11... | collective-permute-start | bytes 98312 | tf_op jit(solution)/shard_map/ppermute | solution.py:286
  31.0 0.9 %collective-permute-done.5 = f32[64,128]{1,0:T(8,128)S(1)} collective-permute-done((f32[64,128]{1,0:T(8,128)S(1)}, f32[64,128]{1,0:T(8,128)S(1)}, u32[]{:S(2)}, u32[]{:S(2)}) %collective-permute-start.5) | collective-permute-done | bytes 32800 | tf_op jit(solution)/shard_map/ppermute | solution.py:286
  31.9 1.5 %collective-permute-done.4 = f32[64,128]{1,0:T(8,128)S(1)} collective-permute-done((f32[64,128]{1,0:T(8,128)S(1)}, f32[64,128]{1,0:T(8,128)S(1)}, u32[]{:S(2)}, u32[]{:S(2)}) %collective-permute-start.4) | collective-permute-done | bytes 32800 | tf_op jit(solution)/shard_map/ppermute | solution.py:286
  33.3 1.8 %collective-permute-start.6 = (f32[64,128]{1,0:T(8,128)S(1)}, f32[64,128]{1,0:T(8,128)S(1)}, u32[]{:S(2)}, u32[]{:S(2)}) collective-permute-start(f32[64,128]{1,0:T(8,128)S(1)} %select_add_fusion.mine_ref), channel_id=1, source_target_pairs={{0,4},{1,5},{2,6},{3,7},{4,0},{5,1},{6,2},{7,3},{8,12},{9,13},{10,... | collective-permute-start | bytes 98312 | tf_op jit(solution)/shard_map/ppermute | solution.py:286
  35.2 0.9 %collective-permute-done.6.other_ref = f32[64,128]{1,0:T(8,128)S(1)} collective-permute-done((f32[64,128]{1,0:T(8,128)S(1)}, f32[64,128]{1,0:T(8,128)S(1)}, u32[]{:S(2)}, u32[]{:S(2)}) %collective-permute-start.6) | collective-permute-done | bytes 32800 | tf_op jit(solution)/shard_map/ppermute | solution.py:286
  36.0 0.7 %unpack.1 = (f32[54,64]{1,0:T(8,128)}, f32[1,64]{1,0:T(1,128)}, f32[64,64]{1,0:T(8,128)}, f32[1,64]{1,0:T(1,128)}) custom-call(f32[64,128]{1,0:T(8,128)S(1)} %select_add_fusion.mine_ref, f32[64,128]{1,0:T(8,128)S(1)} %collective-permute-done.6.other_ref), custom_call_target="tpu_custom_call" | custom-call | tf_op jit(solution)/shard_map/unpack/pallas_call | solution.py:428
  (10 shorter events, 0.0 us)
Async XLA Ops:
  0.6 5.4 %copy-start.1 = (bf16[64,64]{1,0:T(8,128)(2,1)S(1)}, bf16[64,64]{1,0:T(8,128)(2,1)}, u32[]{:S(2)}) copy-start(bf16[64,64]{1,0:T(8,128)(2,1)} %refs_2_.1) | copy-start | bytes 24580
  0.6 10.9 %copy-start = (s32[1,1,32,1024]{3,2,1,0:T(8,128)S(1)}, s32[1,1,32,1024]{3,2,1,0:T(8,128)}, u32[]{:S(2)}) copy-start(s32[1,1,32,1024]{3,2,1,0:T(8,128)} %param.7) | copy-start | bytes 393220
  0.7 10.8 %all-to-all-start = ((f32[8,8,512]{2,1,0:T(8,128)}), f32[8,8,512]{2,1,0:T(8,128)S(1)}, u32[]{:S(2)}, u32[]{:S(2)}) async-start(f32[8,8,512]{2,1,0:T(8,128)} %bitcast.12), calls=%async_computation | async-start | bytes 262144 | tf_op jit(solution)/shard_map/all_to_all | solution.py:386
  6.0 0.7 %copy-start.2 = (bf16[54,64]{1,0:T(8,128)(2,1)S(1)}, bf16[54,64]{1,0:T(8,128)(2,1)}, u32[]{:S(2)}) copy-start(bf16[54,64]{1,0:T(8,128)(2,1)} %refs_0_.1) | copy-start | bytes 20740
  6.0 0.7 %copy-start.3 = (f32[64]{0:T(128)S(1)}, f32[64]{0:T(128)}, u32[]{:S(2)}) copy-start(f32[64]{0:T(128)} %param.9) | copy-start | bytes 772
  6.0 0.7 %copy-start.4 = (f32[64]{0:T(128)S(1)}, f32[64]{0:T(128)}, u32[]{:S(2)}) copy-start(f32[64]{0:T(128)} %param.11) | copy-start | bytes 772
  20.9 1.3 %collective-permute-start = (f32[64,128]{1,0:T(8,128)S(1)}, f32[64,128]{1,0:T(8,128)S(1)}, u32[]{:S(2)}, u32[]{:S(2)}) collective-permute-start(f32[64,128]{1,0:T(8,128)S(1)} %get-tuple-element.21), channel_id=1, source_target_pairs={{0,4},{1,5},{2,6},{3,7},{4,0},{5,1},{6,2},{7,3},{8,12},{9,13},{10,... | collective-permute-start | bytes 98312 | tf_op jit(solution)/shard_map/ppermute | solution.py:286
  22.2 3.9 %collective-permute-start.2 = (f32[64,128]{1,0:T(8,128)S(1)}, f32[64,128]{1,0:T(8,128)S(1)}, u32[]{:S(2)}, u32[]{:S(2)}) collective-permute-start(f32[64,128]{1,0:T(8,128)S(1)} %add.12), channel_id=1, source_target_pairs={{0,8},{1,9},{2,10},{3,11},{4,28},{5,29},{6,30},{7,31},{8,0},{9,1},... | collective-permute-start | bytes 98312 | tf_op jit(solution)/shard_map/ppermute | solution.py:286
  22.7 3.9 %collective-permute-start.1 = (f32[64,128]{1,0:T(8,128)S(1)}, f32[64,128]{1,0:T(8,128)S(1)}, u32[]{:S(2)}, u32[]{:S(2)}) collective-permute-start(f32[64,128]{1,0:T(8,128)S(1)} %add.12), channel_id=1, source_target_pairs={{0,8},{1,9},{2,10},{3,11},{4,20},{5,21},{6,22},{7,23},{8,0},{9,1},... | collective-permute-start | bytes 98312 | tf_op jit(solution)/shard_map/ppermute | solution.py:286
  26.7 1.3 %collective-permute-start.3 = (f32[64,128]{1,0:T(8,128)S(1)}, f32[64,128]{1,0:T(8,128)S(1)}, u32[]{:S(2)}, u32[]{:S(2)}) collective-permute-start(f32[64,128]{1,0:T(8,128)S(1)} %get-tuple-element.27), channel_id=1, source_target_pairs={{0,4},{1,5},{2,6},{3,7},{4,0},{5,1},{6,2},{7,3},{8,12},{9,13},{10,... | collective-permute-start | bytes 98312 | tf_op jit(solution)/shard_map/ppermute | solution.py:286
  27.9 3.9 %collective-permute-start.5 = (f32[64,128]{1,0:T(8,128)S(1)}, f32[64,128]{1,0:T(8,128)S(1)}, u32[]{:S(2)}, u32[]{:S(2)}) collective-permute-start(f32[64,128]{1,0:T(8,128)S(1)} %add.14), channel_id=1, source_target_pairs={{0,8},{1,9},{2,10},{3,11},{4,7},{5,6},{6,5},{7,4},{8,0},{9,1},{10,... | collective-permute-start | bytes 98312 | tf_op jit(solution)/shard_map/ppermute | solution.py:286
  29.4 3.9 %collective-permute-start.4 = (f32[64,128]{1,0:T(8,128)S(1)}, f32[64,128]{1,0:T(8,128)S(1)}, u32[]{:S(2)}, u32[]{:S(2)}) collective-permute-start(f32[64,128]{1,0:T(8,128)S(1)} %add.14), channel_id=1, source_target_pairs={{0,1},{1,0},{2,3},{3,2},{4,6},{5,7},{6,4},{7,5},{8,9},{9,8},{10,11... | collective-permute-start | bytes 98312 | tf_op jit(solution)/shard_map/ppermute | solution.py:286
  33.3 2.7 %collective-permute-start.6 = (f32[64,128]{1,0:T(8,128)S(1)}, f32[64,128]{1,0:T(8,128)S(1)}, u32[]{:S(2)}, u32[]{:S(2)}) collective-permute-start(f32[64,128]{1,0:T(8,128)S(1)} %select_add_fusion.mine_ref), channel_id=1, source_target_pairs={{0,4},{1,5},{2,6},{3,7},{4,0},{5,1},{6,2},{7,3},{8,12},{9,13},{10,... | collective-permute-start | bytes 98312 | tf_op jit(solution)/shard_map/ppermute | solution.py:286

commit v4 on v2

--- a/solution.py
+++ b/solution.py
@@ -113,7 +113,7 @@
     for refs in acts:
         for ref in refs:
             ref[hidden:, :] = jnp.ones((ref.shape[0] - hidden, LANES), jnp.bfloat16)
-    bin_ids = lax.broadcasted_iota(jnp.int32, (bins, LANES), 0)
+    bin_ids = lax.broadcasted_iota(jnp.int32, (bins, LANES), 0).astype(jnp.float32)
 
     def place(n):
         return n // across, pl.ds(n % across * LANES, LANES)
@@ -168,8 +168,9 @@
         partition = jnp.sum(exp_logits, axis=0, keepdims=True)
         is_label = bin_ids == labels_ref[row, lanes]
         sums[row, lanes] = partition
-        picked[row, lanes] = jnp.sum(jnp.where(is_label, logits, 0.0), axis=0, keepdims=True)
-        residual = exp_logits * (scale * inverse(partition)) - jnp.where(is_label, scale, 0.0)
+        chosen = jnp.where(is_label, scale, 0.0)
+        picked[row, lanes] = jnp.sum(chosen * logits, axis=0, keepdims=True) * (1.0 / scale)
+        residual = exp_logits * (scale * inverse(partition)) - chosen
         residuals[(slot - 1) % SLOTS][q][...] = residual.astype(jnp.bfloat16)
         return fold_lanes(residual)
 
@@ -294,7 +295,7 @@
     value = value + sent(cores, (1,))
     for group in groups:
         if len(group) == 2:
-            near, far, last = [sent(group, steps) for steps in ((1, 0), (0, 1), (1, 1))]
+            last, far, near = [sent(group, steps) for steps in ((1, 1), (0, 1), (1, 0))]
             value = (value + near) + (far + last)
         elif group[0][2] == 2:
             value = value + sent(group, (1,))
@@ -381,7 +382,7 @@
     arrived = lax.all_to_all(brick, ("sec", "sp"), split_axis=0, concat_axis=1, tiled=True)
     width = arrived.shape[2]
     arrived = arrived.reshape(sections, -1, width)
-    patch_labels = labels.reshape(labels.shape[2:])
+    patch_labels = labels.reshape(labels.shape[2:]).astype(jnp.float32)
     planes, plane = patch_labels.shape
     hidden, bins = out_weight.shape
     scale = 1.0 / (lax.axis_size("sec") * lax.axis_size("sp") * lax.axis_size("dp") * planes * plane)

time: 36.5 us -> 35.9 us (0.984)
  Pallas kernels: 10.4 us -> 9.84 us
    pallas_call x1, Pallas kernels: 9.38 us -> 8.86 us  [shards(): pl.pallas_call(functools.partial(train_patch, scale), out_shape=(jax.Shap...]
where the time goes in v4:
time: 35.9 us; the launch traced here: 35.6 us
  starting transfers between devices  12.5 us (35%)
  waiting for transfers between devices  11.8 us (33%)
  Pallas kernels  9.84 us (27%)
  between operations  0.74 us (2%)
  local copies, waits for them, and re-layouts  0.7 us (2%)
    pallas_call x1, Pallas kernels, shards(): pl.pallas_call(functools.partial(train_patch, scale), out_shape=(jax.Shap...  8.86 us
    ppermute x8, waiting for transfers between devices, sent(): return lax.ppermute(value, AXES, [(i, target(i)) for i in range(total)])  7.29 us
    ppermute x8, starting transfers between devices, sent(): return lax.ppermute(value, AXES, [(i, target(i)) for i in range(total)])  7.19 us
    all_to_all x1, starting transfers between devices, shards(): lax.all_to_all(brick, ('sec', 'sp'), split_axis=0, concat_axis=1, tiled=T...  5.31 us
    all_to_all x1, waiting for transfers between devices, shards(): lax.all_to_all(brick, ('sec', 'sp'), split_axis=0, concat_axis=1, tiled=T...  4.48 us
  transfers between devices with their start and end apart: 9, of which 8 were waited for; matrix products, arithmetic and copies ran while one was open for 0% of the time, Pallas kernels for 1%

profile of v4, /device:TPU:0, one launch (start us, length us, event | category | flops | bytes accessed | tf_op | source)
XLA Modules:
  0.0 35.6 jit_solution(17015630065831798970)
XLA Ops:
  0.6 5.3 %all-to-all-start = ((f32[8,8,512]{2,1,0:T(8,128)}), f32[8,8,512]{2,1,0:T(8,128)S(1)}, u32[]{:S(2)}, u32[]{:S(2)}) async-start(f32[8,8,512]{2,1,0:T(8,128)} %bitcast.12), calls=%async_computation | async-start | bytes 262144 | tf_op jit(solution)/shard_map/all_to_all | solution.py:382
  6.0 0.0 copy-start.1
  6.0 0.0 copy-start.2
  6.0 0.6 %copy-done = bf16[64,64]{1,0:T(8,128)(2,1)S(1)} copy-done((bf16[64,64]{1,0:T(8,128)(2,1)S(1)}, bf16[64,64]{1,0:T(8,128)(2,1)}, u32[]{:S(2)}) %copy-start) | copy-done | bytes 8216
  6.7 0.0 copy-done.1
  6.7 0.3 prepare.1
  7.0 4.5 %all-to-all-done = f32[8,8,512]{2,1,0:T(8,128)S(1)} async-done(((f32[8,8,512]{2,1,0:T(8,128)}), f32[8,8,512]{2,1,0:T(8,128)S(1)}, u32[]{:S(2)}, u32[]{:S(2)}) %all-to-all-start) | async-done | bytes 131104 | tf_op jit(solution)/shard_map/all_to_all | solution.py:382
  11.5 8.9 %train_patch.1 = (f32[32,1024]{1,0:T(8,128)}, f32[64,128]{1,0:T(8,128)S(1)}) custom-call(f32[2,32,512]{2,1,0:T(8,128)S(1)} %bitcast.9, f32[32,1024]{1,0:T(8,128)S(1)} %convert_bitcast_fusion.labels_ref, bf16[256,144]{1,0:T(8,128)(2,1)S(1)} %get-tuple-element.17.conv_ref, bf16[64,80]{1,0:T(8,128)(2,1)S(1)} %get-tuple-element.18.out_t_ref, ...), custom_call_target="tpu_custom_call" | custom-call | tf_op jit(solution)/shard_map/train_patch/pallas_call | solution.py:396
  20.4 0.1 collective-permute-start
  20.4 1.2 %collective-permute-done = f32[64,128]{1,0:T(8,128)S(1)} collective-permute-done((f32[64,128]{1,0:T(8,128)S(1)}, f32[64,128]{1,0:T(8,128)S(1)}, u32[]{:S(2)}, u32[]{:S(2)}) %collective-permute-start) | collective-permute-done | bytes 32800 | tf_op jit(solution)/shard_map/ppermute | solution.py:293
  21.6 0.6 %collective-permute-start.3 = (f32[64,128]{1,0:T(8,128)S(1)}, f32[64,128]{1,0:T(8,128)S(1)}, u32[]{:S(2)}, u32[]{:S(2)}) collective-permute-start(f32[64,128]{1,0:T(8,128)S(1)} %add.21), channel_id=1, source_target_pairs={{0,24},{1,25},{2,26},{3,27},{4,28},{5,29},{6,30},{7,31},{8,16},{9,... | collective-permute-start | bytes 98312 | tf_op jit(solution)/shard_map/ppermute | solution.py:293
  22.2 1.5 %collective-permute-start.2 = (f32[64,128]{1,0:T(8,128)S(1)}, f32[64,128]{1,0:T(8,128)S(1)}, u32[]{:S(2)}, u32[]{:S(2)}) collective-permute-start(f32[64,128]{1,0:T(8,128)S(1)} %add.21), channel_id=1, source_target_pairs={{0,16},{1,17},{2,18},{3,19},{4,20},{5,21},{6,22},{7,23},{8,24},{9,... | collective-permute-start | bytes 98312 | tf_op jit(solution)/shard_map/ppermute | solution.py:293
  23.7 1.5 %collective-permute-start.1 = (f32[64,128]{1,0:T(8,128)S(1)}, f32[64,128]{1,0:T(8,128)S(1)}, u32[]{:S(2)}, u32[]{:S(2)}) collective-permute-start(f32[64,128]{1,0:T(8,128)S(1)} %add.21), channel_id=1, source_target_pairs={{0,8},{1,9},{2,10},{3,11},{4,12},{5,13},{6,14},{7,15},{8,0},{9,1},... | collective-permute-start | bytes 98312 | tf_op jit(solution)/shard_map/ppermute | solution.py:293
  25.1 1.4 %collective-permute-done.3 = f32[64,128]{1,0:T(8,128)S(1)} collective-permute-done((f32[64,128]{1,0:T(8,128)S(1)}, f32[64,128]{1,0:T(8,128)S(1)}, u32[]{:S(2)}, u32[]{:S(2)}) %collective-permute-start.3) | collective-permute-done | bytes 32800 | tf_op jit(solution)/shard_map/ppermute | solution.py:293
  26.6 1.0 %collective-permute-done.1 = f32[64,128]{1,0:T(8,128)S(1)} collective-permute-done((f32[64,128]{1,0:T(8,128)S(1)}, f32[64,128]{1,0:T(8,128)S(1)}, u32[]{:S(2)}, u32[]{:S(2)}) %collective-permute-start.1) | collective-permute-done | bytes 32800 | tf_op jit(solution)/shard_map/ppermute | solution.py:293
  27.6 0.6 %collective-permute-start.6 = (f32[64,128]{1,0:T(8,128)S(1)}, f32[64,128]{1,0:T(8,128)S(1)}, u32[]{:S(2)}, u32[]{:S(2)}) collective-permute-start(f32[64,128]{1,0:T(8,128)S(1)} %add_add_fusion.1), channel_id=1, source_target_pairs={{0,16},{1,17},{2,18},{3,19},{4,7},{5,6},{6,5},{7,4},{8,24},{9,25},... | collective-permute-start | bytes 98312 | tf_op jit(solution)/shard_map/ppermute | solution.py:293
  28.2 1.5 %collective-permute-start.5 = (f32[64,128]{1,0:T(8,128)S(1)}, f32[64,128]{1,0:T(8,128)S(1)}, u32[]{:S(2)}, u32[]{:S(2)}) collective-permute-start(f32[64,128]{1,0:T(8,128)S(1)} %add_add_fusion.1), channel_id=1, source_target_pairs={{0,16},{1,17},{2,18},{3,19},{4,6},{5,7},{6,4},{7,5},{8,24},{9,25},... | collective-permute-start | bytes 98312 | tf_op jit(solution)/shard_map/ppermute | solution.py:293
  29.7 1.5 %collective-permute-start.4 = (f32[64,128]{1,0:T(8,128)S(1)}, f32[64,128]{1,0:T(8,128)S(1)}, u32[]{:S(2)}, u32[]{:S(2)}) collective-permute-start(f32[64,128]{1,0:T(8,128)S(1)} %add_add_fusion.1), channel_id=1, source_target_pairs={{0,8},{1,9},{2,10},{3,11},{4,5},{5,4},{6,7},{7,6},{8,0},{9,1},{10,... | collective-permute-start | bytes 98312 | tf_op jit(solution)/shard_map/ppermute | solution.py:293
  31.1 0.4 %collective-permute-done.6 = f32[64,128]{1,0:T(8,128)S(1)} collective-permute-done((f32[64,128]{1,0:T(8,128)S(1)}, f32[64,128]{1,0:T(8,128)S(1)}, u32[]{:S(2)}, u32[]{:S(2)}) %collective-permute-start.6) | collective-permute-done | bytes 32800 | tf_op jit(solution)/shard_map/ppermute | solution.py:293
  31.6 0.6 %collective-permute-done.5 = f32[64,128]{1,0:T(8,128)S(1)} collective-permute-done((f32[64,128]{1,0:T(8,128)S(1)}, f32[64,128]{1,0:T(8,128)S(1)}, u32[]{:S(2)}, u32[]{:S(2)}) %collective-permute-start.5) | collective-permute-done | bytes 32800 | tf_op jit(solution)/shard_map/ppermute | solution.py:293
  32.1 1.5 %collective-permute-done.4 = f32[64,128]{1,0:T(8,128)S(1)} collective-permute-done((f32[64,128]{1,0:T(8,128)S(1)}, f32[64,128]{1,0:T(8,128)S(1)}, u32[]{:S(2)}, u32[]{:S(2)}) %collective-permute-start.4) | collective-permute-done | bytes 32800 | tf_op jit(solution)/shard_map/ppermute | solution.py:293
  33.6 0.1 collective-permute-start.7
  33.7 1.2 %collective-permute-done.7.back_ref = f32[64,128]{1,0:T(8,128)S(1)} collective-permute-done((f32[64,128]{1,0:T(8,128)S(1)}, f32[64,128]{1,0:T(8,128)S(1)}, u32[]{:S(2)}, u32[]{:S(2)}) %collective-permute-start.7) | collective-permute-done | bytes 32800 | tf_op jit(solution)/shard_map/ppermute | solution.py:293
  34.9 0.7 %unpack.1 = (f32[54,64]{1,0:T(8,128)}, f32[1,64]{1,0:T(1,128)}, f32[64,64]{1,0:T(8,128)}, f32[1,64]{1,0:T(1,128)}) custom-call(f32[64,128]{1,0:T(8,128)S(1)} %add_add_fusion.mine_ref, f32[64,128]{1,0:T(8,128)S(1)} %collective-permute-done.7.back_ref, f32[1,128]{1,0:T(1,128)S(1)} %broadcast_in_dim.3.mask_ref), custom_call_target="tpu_custom_call" | custom-call | tf_op jit(solution)/shard_map/unpack/pallas_call | solution.py:424
  (12 shorter events, 0.1 us)
Async XLA Ops:
  0.6 5.3 %copy-start.4 = (s32[1,1,32,1024]{3,2,1,0:T(8,128)S(1)}, s32[1,1,32,1024]{3,2,1,0:T(8,128)}, u32[]{:S(2)}) copy-start(s32[1,1,32,1024]{3,2,1,0:T(8,128)} %param.7) | copy-start | bytes 393220
  0.6 10.8 %all-to-all-start = ((f32[8,8,512]{2,1,0:T(8,128)}), f32[8,8,512]{2,1,0:T(8,128)S(1)}, u32[]{:S(2)}, u32[]{:S(2)}) async-start(f32[8,8,512]{2,1,0:T(8,128)} %bitcast.12), calls=%async_computation | async-start | bytes 262144 | tf_op jit(solution)/shard_map/all_to_all | solution.py:382
  6.0 0.7 %copy-start = (bf16[64,64]{1,0:T(8,128)(2,1)S(1)}, bf16[64,64]{1,0:T(8,128)(2,1)}, u32[]{:S(2)}) copy-start(bf16[64,64]{1,0:T(8,128)(2,1)} %refs_2_.1) | copy-start | bytes 24580
  6.0 0.7 %copy-start.1 = (bf16[54,64]{1,0:T(8,128)(2,1)S(1)}, bf16[54,64]{1,0:T(8,128)(2,1)}, u32[]{:S(2)}) copy-start(bf16[54,64]{1,0:T(8,128)(2,1)} %refs_0_.1) | copy-start | bytes 20740
  6.0 0.7 %copy-start.2 = (f32[64]{0:T(128)S(1)}, f32[64]{0:T(128)}, u32[]{:S(2)}) copy-start(f32[64]{0:T(128)} %param.9) | copy-start | bytes 772
  6.0 0.7 %copy-start.3 = (f32[64]{0:T(128)S(1)}, f32[64]{0:T(128)}, u32[]{:S(2)}) copy-start(f32[64]{0:T(128)} %param.11) | copy-start | bytes 772
  20.4 1.3 %collective-permute-start = (f32[64,128]{1,0:T(8,128)S(1)}, f32[64,128]{1,0:T(8,128)S(1)}, u32[]{:S(2)}, u32[]{:S(2)}) collective-permute-start(f32[64,128]{1,0:T(8,128)S(1)} %get-tuple-element.21), channel_id=1, source_target_pairs={{0,4},{1,5},{2,6},{3,7},{4,0},{5,1},{6,2},{7,3},{8,12},{9,13},{10,... | collective-permute-start | bytes 98312 | tf_op jit(solution)/shard_map/ppermute | solution.py:293
  21.6 4.9 %collective-permute-start.3 = (f32[64,128]{1,0:T(8,128)S(1)}, f32[64,128]{1,0:T(8,128)S(1)}, u32[]{:S(2)}, u32[]{:S(2)}) collective-permute-start(f32[64,128]{1,0:T(8,128)S(1)} %add.21), channel_id=1, source_target_pairs={{0,24},{1,25},{2,26},{3,27},{4,28},{5,29},{6,30},{7,31},{8,16},{9,... | collective-permute-start | bytes 98312 | tf_op jit(solution)/shard_map/ppermute | solution.py:293
  22.2 4.4 %collective-permute-start.2 = (f32[64,128]{1,0:T(8,128)S(1)}, f32[64,128]{1,0:T(8,128)S(1)}, u32[]{:S(2)}, u32[]{:S(2)}) collective-permute-start(f32[64,128]{1,0:T(8,128)S(1)} %add.21), channel_id=1, source_target_pairs={{0,16},{1,17},{2,18},{3,19},{4,20},{5,21},{6,22},{7,23},{8,24},{9,... | collective-permute-start | bytes 98312 | tf_op jit(solution)/shard_map/ppermute | solution.py:293
  23.7 3.9 %collective-permute-start.1 = (f32[64,128]{1,0:T(8,128)S(1)}, f32[64,128]{1,0:T(8,128)S(1)}, u32[]{:S(2)}, u32[]{:S(2)}) collective-permute-start(f32[64,128]{1,0:T(8,128)S(1)} %add.21), channel_id=1, source_target_pairs={{0,8},{1,9},{2,10},{3,11},{4,12},{5,13},{6,14},{7,15},{8,0},{9,1},... | collective-permute-start | bytes 98312 | tf_op jit(solution)/shard_map/ppermute | solution.py:293
  27.6 4.0 %collective-permute-start.6 = (f32[64,128]{1,0:T(8,128)S(1)}, f32[64,128]{1,0:T(8,128)S(1)}, u32[]{:S(2)}, u32[]{:S(2)}) collective-permute-start(f32[64,128]{1,0:T(8,128)S(1)} %add_add_fusion.1), channel_id=1, source_target_pairs={{0,16},{1,17},{2,18},{3,19},{4,7},{5,6},{6,5},{7,4},{8,24},{9,25},... | collective-permute-start | bytes 98312 | tf_op jit(solution)/shard_map/ppermute | solution.py:293
  28.2 3.9 %collective-permute-start.5 = (f32[64,128]{1,0:T(8,128)S(1)}, f32[64,128]{1,0:T(8,128)S(1)}, u32[]{:S(2)}, u32[]{:S(2)}) collective-permute-start(f32[64,128]{1,0:T(8,128)S(1)} %add_add_fusion.1), channel_id=1, source_target_pairs={{0,16},{1,17},{2,18},{3,19},{4,6},{5,7},{6,4},{7,5},{8,24},{9,25},... | collective-permute-start | bytes 98312 | tf_op jit(solution)/shard_map/ppermute | solution.py:293
  29.7 3.9 %collective-permute-start.4 = (f32[64,128]{1,0:T(8,128)S(1)}, f32[64,128]{1,0:T(8,128)S(1)}, u32[]{:S(2)}, u32[]{:S(2)}) collective-permute-start(f32[64,128]{1,0:T(8,128)S(1)} %add_add_fusion.1), channel_id=1, source_target_pairs={{0,8},{1,9},{2,10},{3,11},{4,5},{5,4},{6,7},{7,6},{8,0},{9,1},{10,... | collective-permute-start | bytes 98312 | tf_op jit(solution)/shard_map/ppermute | solution.py:293
  33.6 1.3 %collective-permute-start.7 = (f32[64,128]{1,0:T(8,128)S(1)}, f32[64,128]{1,0:T(8,128)S(1)}, u32[]{:S(2)}, u32[]{:S(2)}) collective-permute-start(f32[64,128]{1,0:T(8,128)S(1)} %add_add_fusion.mine_ref), channel_id=1, source_target_pairs={{0,4},{1,5},{2,6},{3,7},{4,0},{5,1},{6,2},{7,3},{8,12},{9,13},{10,... | collective-permute-start | bytes 98312 | tf_op jit(solution)/shard_map/ppermute | solution.py:293
